TPU v7x, 128 devices: a whole 4x4x4 slice. The times are simulated.
128 devices in a mesh: dp: 8 (over x, z_lo), tensor: 16 (over z_hi, y, core).
Axes of the slice: x: 4, y: 4, z: 4 (z_hi: 2, z_lo: 2; z = z_hi * 2 + z_lo), core: 2. Of those that a mesh axis runs over, the one named last changes fastest.
Arguments:
- text_grads: bfloat16 [8, 8192, 2048], P('dp', 'tensor'), may hold values from -6 to 6
- text_master: float32 [8192, 2048], P('tensor', 'dp'), may hold values from -2 to 2
- text_moment: float32 [8192, 2048], P('tensor', 'dp'), may hold values from -4 to 4
- text_second: float32 [8192, 2048], P('tensor', 'dp'), may hold values from 0.01 to 1
- text_ref: float32 [8192, 2048], P('tensor', 'dp'), may hold values from -2 to 2
- vision_grads: bfloat16 [128, 2, 1280, 1280], P(('dp', 'tensor')), may hold values from -6 to 6
- vision_master: float32 [2, 1280, 1280], P(None, ('dp', 'tensor')), may hold values from -2 to 2
- vision_moment: float32 [2, 1280, 1280], P(None, ('dp', 'tensor')), may hold values from -4 to 4
- vision_second: float32 [2, 1280, 1280], P(None, ('dp', 'tensor')), may hold values from 0.01 to 1
- vision_ref: float32 [2, 1280, 1280], P(None, ('dp', 'tensor')), may hold values from -2 to 2
Outputs:
- text_master_new: float32 [8192, 2048], P('tensor', 'dp')
- text_moment_new: float32 [8192, 2048], P('tensor', 'dp')
- text_second_new: float32 [8192, 2048], P('tensor', 'dp')
- text_ref_new: float32 [8192, 2048], P('tensor', 'dp')
- text_weights: bfloat16 [8192, 2048], P('tensor')
- vision_master_new: float32 [2, 1280, 1280], P(None, ('dp', 'tensor'))
- vision_moment_new: float32 [2, 1280, 1280], P(None, ('dp', 'tensor'))
- vision_second_new: float32 [2, 1280, 1280], P(None, ('dp', 'tensor'))
- vision_ref_new: float32 [2, 1280, 1280], P(None, ('dp', 'tensor'))
- vision_weights: bfloat16 [2, 1280, 1280], replicated
All inputs are finite; a program needn't handle non-finite values.
Results may differ from a plain program's by a relative error of at most 0.012.
Values may be sent and summed in bfloat16 or wider, within the bound.
A program may use at most 128 MiB of HBM per device.

v0:
```python
import jax
import jax.numpy as jnp
from jax import lax
from jax.sharding import PartitionSpec as P

beta_one = 0.9
beta_two = 0.95
correct_one = 1.0 - 0.9**10
correct_two = 1.0 - 0.95**10
learn_rate = 0.01
decay_rate = 0.1
blend_rate = 0.6


def adam_step(grad, moment, second, master, refcopy):
    moment_new = beta_one * moment + (1.0 - beta_one) * grad
    second_new = beta_two * second + (1.0 - beta_two) * grad * grad
    update = moment_new / correct_one / (jnp.sqrt(second_new / correct_two) + 1e-08)
    master_new = master - learn_rate * (update + decay_rate * master)
    ref_new = blend_rate * master_new + (1.0 - blend_rate) * refcopy
    return (master_new, moment_new, second_new, ref_new, master_new.astype(jnp.bfloat16))


def body(
    text_grads,
    text_master,
    text_moment,
    text_second,
    text_ref,
    vision_grads,
    vision_master,
    vision_moment,
    vision_second,
    vision_ref,
):
    vision_total = lax.psum_scatter(
        vision_grads[0].astype(jnp.float32), ("dp", "tensor"), scatter_dimension=1, tiled=True
    )
    text_total = lax.psum_scatter(
        text_grads[0].astype(jnp.float32).astype(jnp.bfloat16),
        "dp",
        scatter_dimension=1,
        tiled=True,
    ).astype(jnp.float32)
    text_out = adam_step(text_total, text_moment, text_second, text_master, text_ref)
    vision_out = adam_step(vision_total, vision_moment, vision_second, vision_master, vision_ref)
    text_full = lax.all_gather(text_out[4], "dp", axis=1, tiled=True)
    vision_full = lax.all_gather(vision_out[4], ("dp", "tensor"), axis=1, tiled=True)
    return (
        text_out[0],
        text_out[1],
        text_out[2],
        text_out[3],
        text_full,
        vision_out[0],
        vision_out[1],
        vision_out[2],
        vision_out[3],
        vision_full,
    )


def solution(mesh):
    return jax.shard_map(
        body,
        mesh=mesh,
        in_specs=(
            P("dp", "tensor", None),
            P("tensor", "dp"),
            P("tensor", "dp"),
            P("tensor", "dp"),
            P("tensor", "dp"),
            P(("dp", "tensor"), None, None, None),
            P(None, ("dp", "tensor"), None),
            P(None, ("dp", "tensor"), None),
            P(None, ("dp", "tensor"), None),
            P(None, ("dp", "tensor"), None),
        ),
        out_specs=(
            P("tensor", "dp"),
            P("tensor", "dp"),
            P("tensor", "dp"),
            P("tensor", "dp"),
            P("tensor", None),
            P(None, ("dp", "tensor"), None),
            P(None, ("dp", "tensor"), None),
            P(None, ("dp", "tensor"), None),
            P(None, ("dp", "tensor"), None),
            P(),
        ),
        check_vma=False,
    )
```

profile of v0, /device:TPU:1, one launch (start us, length us, event | category | flops | bytes accessed | tf_op | source)
XLA Modules:
  0.0 459.5 jit_solution(10717325622877719342)
XLA Ops:
  8.0 0.0 reduce-scatter.2.cloned.1.call-start
  8.1 0.7 reduce-scatter.2.cloned.1.call-update
  8.7 0.0 all-reduce.3.cloned.1.call-start
  8.8 28.6 %bitcast_convert_fusion = f32[2,1280,1280]{2,0,1:T(2,128)} fusion(bf16[1,2,1280,1280]{3,2,1,0:T(8,128)(2,1)} %param.15), kind=kLoop, calls=%fused_computation | loop fusion | flops 3276800 | bytes 19660800 | tf_op jit(solution)/shard_map/convert_element_type | solution.py:37
  37.4 0.0 copy-start.4
  37.4 0.0 copy-start.8
  37.4 0.0 copy-start.9
  37.4 0.0 copy-start.10
  37.4 0.0 copy-start.5
  37.5 0.0 copy-start.7
  37.5 0.0 all-reduce.3.cloned.1.call-update
  37.5 0.0 all-gather.3.cloned.1.call-start
  37.5 31.6 %reduce-scatter.2.cloned.1.call-done = bf16[512,256]{1,0:T(8,128)(2,1)} async-done(((bf16[512,2048]{1,0:T(8,128)(2,1)}), bf16[512,256]{1,0:T(8,128)(2,1)}) %reduce-scatter.2.cloned.1.call-update) | async-done | bytes 262160 | tf_op jit(solution)/shard_map/reduce_scatter | solution.py:39
  69.1 0.0 copy-done.2
  69.1 0.0 copy-done.3
  69.1 0.0 copy-done.4
  69.1 2.3 fusion.5
  71.4 0.0 all-gather.3.cloned.1.call-update
  71.4 0.0 all-gather.5.cloned.1.call-start
  71.5 171.4 %all-reduce.3.cloned.1.call-done = f32[2,1280,1280]{2,0,1:T(2,128)} async-done(((f32[2,1280,1280]{2,0,1:T(2,128)}), f32[2,1280,1280]{2,0,1:T(2,128)}) %all-reduce.3.cloned.1.call-update) | async-done | bytes 13107216
  242.8 0.0 copy-done.8
  242.8 0.0 copy-done.9
  242.9 0.0 copy-done.10
  242.9 1.9 fusion.3
  244.8 0.0 all-gather.5.cloned.1.call-update
  244.8 0.0 copy-done.5
  244.8 0.9 multiply_add_fusion
  245.7 0.0 copy-done.7
  245.7 0.7 multiply_add_fusion.1
  246.4 198.1 %all-gather.5.cloned.1.call-done = bf16[2,1280,1280]{2,0,1:T(2,128)(2,1)} async-done(((bf16[2,10,1280]{2,0,1:T(2,128)(2,1)}), bf16[2,1280,1280]{2,0,1:T(2,128)(2,1)}) %all-gather.5.cloned.1.call-update) | async-done | bytes 6553616 | tf_op jit(solution)/shard_map/all_gather | solution.py:48
  444.6 6.5 %copy.23 = bf16[2,1280,1280]{2,1,0:T(8,128)(2,1)} copy(bf16[2,1280,1280]{2,0,1:T(2,128)(2,1)} %all-gather.5.cloned.1.call-done) | data formatting | bytes 13107200
  451.1 1.3 copy.27
  (9 shorter events, 0.0 us)
Async XLA Ops:
  8.0 61.1 %reduce-scatter.2.cloned.1.call-start = ((), (), s32[]{:S(2)}) async-start(), calls=%async_computation.1 | async-start | bytes 2359296 | tf_op jit(solution)/shard_map/reduce_scatter | solution.py:39
  8.7 234.1 %all-reduce.3.cloned.1.call-start = ((), (), s32[]{:S(2)}) async-start(), calls=%async_computation.4 | async-start | bytes 26214400
  37.4 31.7 %copy-start.2 = (f32[512,256]{1,0:T(8,128)S(1)}, f32[512,256]{1,0:T(8,128)}, u32[]{:S(2)}) copy-start(f32[512,256]{1,0:T(8,128)} %param.11) | copy-start | bytes 1572868
  37.4 31.7 %copy-start.3 = (f32[512,256]{1,0:T(8,128)S(1)}, f32[512,256]{1,0:T(8,128)}, u32[]{:S(2)}) copy-start(f32[512,256]{1,0:T(8,128)} %param.12) | copy-start | bytes 1572868
  37.4 31.7 %copy-start.4 = (f32[512,256]{1,0:T(8,128)S(1)}, f32[512,256]{1,0:T(8,128)}, u32[]{:S(2)}) copy-start(f32[512,256]{1,0:T(8,128)} %param.13) | copy-start | bytes 1572868
  37.4 205.4 %copy-start.8 = (f32[2,10,1280]{2,0,1:T(2,128)S(1)}, f32[2,10,1280]{2,0,1:T(2,128)}, u32[]{:S(2)}) copy-start(f32[2,10,1280]{2,0,1:T(2,128)} %param.16) | copy-start | bytes 307204
  37.4 205.4 %copy-start.9 = (f32[2,10,1280]{2,0,1:T(2,128)S(1)}, f32[2,10,1280]{2,0,1:T(2,128)}, u32[]{:S(2)}) copy-start(f32[2,10,1280]{2,0,1:T(2,128)} %param.17) | copy-start | bytes 307204
  37.4 205.4 %copy-start.10 = (f32[2,10,1280]{2,0,1:T(2,128)S(1)}, f32[2,10,1280]{2,0,1:T(2,128)}, u32[]{:S(2)}) copy-start(f32[2,10,1280]{2,0,1:T(2,128)} %param.18) | copy-start | bytes 307204
  37.4 207.4 %copy-start.5 = (f32[512,256]{1,0:T(8,128)S(1)}, f32[512,256]{1,0:T(8,128)}, u32[]{:S(2)}) copy-start(f32[512,256]{1,0:T(8,128)} %param.14) | copy-start | bytes 1572868
  37.5 208.3 %copy-start.7 = (f32[2,10,1280]{2,0,1:T(2,128)S(1)}, f32[2,10,1280]{2,0,1:T(2,128)}, u32[]{:S(2)}) copy-start(f32[2,10,1280]{2,0,1:T(2,128)} %param.19) | copy-start | bytes 307204
  37.5 209.0 %all-gather.3.cloned.1.call-start = ((), (), s32[]{:S(2)}) async-start(), calls=%async_computation.2 | async-start | bytes 2359296 | tf_op jit(solution)/shard_map/all_gather | solution.py:47
  71.4 379.7 %copy-start = (f32[512,256]{1,0:T(8,128)}, f32[512,256]{1,0:T(8,128)S(1)}, u32[]{:S(2)}) copy-start(f32[512,256]{1,0:T(8,128)S(1)} %get-tuple-element.38) | copy-start | bytes 1572868
  71.4 373.2 %all-gather.5.cloned.1.call-start = ((), (), s32[]{:S(2)}) async-start(), calls=%async_computation.3 | async-start | bytes 6604800 | tf_op jit(solution)/shard_map/all_gather | solution.py:48
  244.8 206.3 %copy-start.6 = (f32[2,10,1280]{2,0,1:T(2,128)}, f32[2,10,1280]{2,0,1:T(2,128)S(1)}, u32[]{:S(2)}) copy-start(f32[2,10,1280]{2,0,1:T(2,128)S(1)} %get-tuple-element.43) | copy-start | bytes 307204
  246.4 204.6 %copy-start.1 = (bf16[512,2048]{1,0:T(8,128)(2,1)S(1)}, bf16[512,2048]{1,0:T(8,128)(2,1)}, u32[]{:S(2)}) copy-start(bf16[512,2048]{1,0:T(8,128)(2,1)} %all-gather.3.cloned.1.call-done) | copy-start | bytes 6291460
Sparse Core Ops, SparseCore 0:
  11.2 57.8 reduce-scatter.1
  71.5 63.6 all-gather.2
  244.9 199.5 all-gather.4
Sparse Core Ops, SparseCore 1:
  37.6 205.2 all-reduce.2
where the time goes:
time: 460 us
  waiting for transfers between devices  402 us (87%)
  other arithmetic  34.4 us (7%)
  between operations  15.3 us (3%)
  local copies, waits for them, and re-layouts  7.85 us (2%)
    all_gather x1, waiting for transfers between devices, body(): lax.all_gather(vision_out[4], ('dp', 'tensor'), axis=1, tiled=True)  198 us
    unnamed x5, waiting for transfers between devices  172 us
    reduce_scatter x1, waiting for transfers between devices, body(): lax.psum_scatter(text_grads[0].astype(jnp.float32).astype(jnp.bfloat16),...  31.6 us
    convert_element_type x1, other arithmetic, body(): vision_grads[0].astype(jnp.float32)  28.6 us
  transfers between devices with their start and end apart: 4, of which 3 were waited for; matrix products, arithmetic and copies ran while one was open for 7% of the time, Pallas kernels for 0%

commit v1 on v0

v1 whole, which is shorter than its diff:
```python
import functools

import jax
import jax.numpy as jnp
from jax import lax
from jax.experimental import pallas as pl
from jax.experimental.pallas import tpu as pltpu
from jax.sharding import PartitionSpec as P

MESH = pl.DeviceIdType.MESH
BF16, F32 = jnp.bfloat16, jnp.float32

beta_one = 0.9
beta_two = 0.95
correct_one = 1.0 - 0.9**10
correct_two = 1.0 - 0.95**10
learn_rate = 0.01
decay_rate = 0.1
blend_rate = 0.6

GROUPS = 16
ROWS = 80
COLS = 256
OPP, RIGHT, LEFT, REST, OWN = range(5)


def adam_step(grad, moment, second, master, refcopy):
    moment_new = beta_one * moment + (1.0 - beta_one) * grad
    second_new = beta_two * second + (1.0 - beta_two) * grad * grad
    update = moment_new / correct_one / (jnp.sqrt(second_new / correct_two) + 1e-08)
    master_new = master - learn_rate * (update + decay_rate * master)
    ref_new = blend_rate * master_new + (1.0 - blend_rate) * refcopy
    return (master_new, moment_new, second_new, ref_new, master_new.astype(BF16))


def place():
    dp, tensor = lax.axis_index("dp"), lax.axis_index("tensor")
    x = dp // 2
    z = (tensor // 8) * 2 + dp % 2
    y = (tensor % 8) // 2
    return x, y, z, tensor % 2


def device(x, y, z, core):
    return (x * 2 + z % 2, (z // 2) * 8 + y * 2 + core)


def group_of(x, z):
    return x * 4 + (z % 2) * 2 + z // 2


def plane_partner(x, z, k):
    return (x + k // 4) % 4, (z + k % 4) % 4


def line_partner(y, core, i):
    return (y + i // 2) % 4, (core + i % 2) % 2


def first_row(y):
    return pl.multiple_of(8 * ((5 * y) // 2), 8)


def remote(src, dst, send, recv, to):
    return pltpu.make_async_remote_copy(
        src_ref=src, dst_ref=dst, send_sem=send, recv_sem=recv, device_id=to, device_id_type=MESH
    )


def loop(first, last, step):
    def run(i, carry):
        step(i)
        return carry

    lax.fori_loop(first, last, run, 0)


def greet(x, y, z, core):
    barrier = pltpu.get_barrier_semaphore()

    def plane(k):
        px, pz = plane_partner(x, z, k)
        pl.semaphore_signal(barrier, inc=1, device_id=device(px, y, pz, core), device_id_type=MESH)

    def line(i):
        py, pc = line_partner(y, core, i)
        pl.semaphore_signal(barrier, inc=1, device_id=device(x, py, z, pc), device_id_type=MESH)

    loop(1, GROUPS, plane)
    loop(1, 8, line)
    pl.semaphore_wait(barrier, GROUPS - 1 + 7)


def scatter_kernel(
    text_hbm, vision_hbm, text_out, vision_out,
    mine, other, paired, over_a, over_b, from_left, from_right, total, plane_in, rest_in, rest_part, rest_line,
    sums, rest_sums, windows, text_own, text_in,
    load_sem, own_sem, pair_s, pair_r, y_s, y_r, plane_s, plane_r, rest_s, rest_r, rest_y_s, rest_y_r,
    win_s, win_r, text_s, text_r,
):
    x, y, z, core = place()
    dp = x * 2 + z % 2
    group = group_of(x, z)
    blocks = [(y + 2) % 4, (y + 1) % 4, (y + 3) % 4, 4, y]

    def loads(role):
        cols = pl.ds(pl.multiple_of(blocks[role] * COLS, COLS), COLS)
        return (
            pltpu.make_async_copy(vision_hbm.at[1 - core, :, :, cols], other.at[role], load_sem.at[role, 0]),
            pltpu.make_async_copy(vision_hbm.at[core, :, :, cols], mine.at[role], load_sem.at[role, 1]),
        )

    for role in (OPP, RIGHT, LEFT, REST, OWN):
        for copy in loads(role):
            copy.start()
    own_text = pltpu.make_async_copy(
        text_hbm.at[:, pl.ds(pl.multiple_of(dp * COLS, COLS), COLS)], text_own, own_sem
    )
    own_text.start()

    greet(x, y, z, core)

    def pair(role):
        return remote(other.at[role], paired.at[role], pair_s.at[role], pair_r.at[role], device(x, y, z, 1 - core))

    def text_copy(k):
        to = (dp + k) % 8
        return remote(
            text_hbm.at[:, pl.ds(pl.multiple_of(to * COLS, COLS), COLS)], text_in.at[k], text_s.at[k], text_r.at[k],
            (to, lax.axis_index("tensor")),
        )

    for role in (OPP, RIGHT, LEFT, REST, OWN):
        loads(role)[0].wait()
        pair(role).start()

    loop(1, 8, lambda k: text_copy(k).start())

    def add_pair(role):
        loads(role)[1].wait()
        pair(role).wait_recv()

        def add(g):
            mine[role, g] = mine[role, g] + paired[role, g]

        loop(0, GROUPS, add)

    right, left = device(x, (y + 1) % 4, z, core), device(x, (y + 3) % 4, z, core)
    half_a, half_b = pl.ds(0, 8), pl.ds(8, 8)
    along = [
        remote(mine.at[OPP, half_a], over_a, y_s.at[0], y_r.at[0], right),
        remote(mine.at[OPP, half_b], over_b, y_s.at[1], y_r.at[1], left),
        remote(mine.at[RIGHT, half_b], from_left.at[half_b], y_s.at[2], y_r.at[2], right),
        remote(mine.at[LEFT, half_a], from_right.at[half_a], y_s.at[3], y_r.at[3], left),
        remote(mine.at[RIGHT, half_a], from_left.at[half_a], y_s.at[4], y_r.at[4], right),
        remote(mine.at[LEFT, half_b], from_right.at[half_b], y_s.at[5], y_r.at[5], left),
    ]
    add_pair(OPP)
    along[0].start()
    along[1].start()
    add_pair(RIGHT)
    along[2].start()
    add_pair(LEFT)
    along[3].start()

    def rest_copy(k):
        px, pz = plane_partner(x, z, k)
        return remote(
            mine.at[REST, group_of(px, pz)], rest_in.at[k], rest_s.at[k], rest_r.at[k], device(px, y, pz, core)
        )

    add_pair(REST)
    loop(1, GROUPS, lambda k: rest_copy(k).start())
    add_pair(OWN)

    along[0].wait_recv()

    def add_a(g):
        mine[RIGHT, g] = mine[RIGHT, g] + over_a[g]

    loop(0, 8, add_a)
    along[4].start()
    along[1].wait_recv()

    def add_b(g):
        mine[LEFT, 8 + g] = mine[LEFT, 8 + g] + over_b[g]

    loop(0, 8, add_b)
    along[5].start()

    for copy in along[2:]:
        copy.wait_recv()

    def add_line(g):
        total[g] = (
            mine[OWN, g].astype(F32) + from_left[g].astype(F32) + from_right[g].astype(F32)
        ).astype(BF16)

    loop(0, GROUPS, add_line)

    def plane_copy(k):
        px, pz = plane_partner(x, z, k)
        return remote(total.at[group_of(px, pz)], plane_in.at[k], plane_s.at[k], plane_r.at[k], device(px, y, pz, core))

    loop(1, GROUPS, lambda k: plane_copy(k).start())

    loop(1, GROUPS, lambda k: rest_copy(k).wait_recv())
    acc = mine[REST, group].astype(F32)
    for k in range(1, GROUPS):
        acc = acc + rest_in[k].astype(F32)
    rest_part[...] = acc.astype(BF16)

    def rest_line_copy(k):
        return remote(
            rest_part, rest_line.at[k], rest_y_s.at[k], rest_y_r.at[k], device(x, (y + k) % 4, z, core)
        )

    for k in range(1, 4):
        rest_line_copy(k).start()

    own_text.wait()
    loop(1, 8, lambda k: text_copy(k).wait_recv())

    def add_text(i):
        rows = pl.ds(pl.multiple_of(i * 32, 32), 32)
        acc = text_own[rows].astype(F32)
        for k in range(1, 8):
            acc = acc + text_in[k, rows].astype(F32)
        text_out[rows] = acc

    loop(0, 16, add_text)

    for k in range(1, 4):
        rest_line_copy(k).wait_recv()
    acc = rest_part[...].astype(F32)
    for k in range(1, 4):
        acc = acc + rest_line[k].astype(F32)
    rest_sums[...] = acc
    own_rows = pl.ds(first_row(y), 24)
    windows[core, 4] = rest_sums[own_rows, :]
    rest_win = remote(
        rest_sums.at[own_rows], windows.at[core, 4], win_s.at[0], win_r.at[0], device(x, y, z, 1 - core)
    )
    rest_win.start()

    loop(1, GROUPS, lambda k: plane_copy(k).wait_recv())
    acc = total[group].astype(F32)
    for k in range(1, GROUPS):
        acc = acc + plane_in[k].astype(F32)
    sums[...] = acc

    def win_copy(i):
        py, pc = line_partner(y, core, i)
        return remote(
            sums.at[pl.ds(first_row(py), 24)], windows.at[core, y], win_s.at[i], win_r.at[i], device(x, py, z, pc)
        )

    loop(1, 8, lambda i: win_copy(i).start())
    windows[core, y] = sums[own_rows, :]

    for role in (OPP, RIGHT, LEFT, REST, OWN):
        pair(role).wait_send()
    for copy in along:
        copy.wait_send()
    loop(1, 8, lambda k: text_copy(k).wait_send())
    loop(1, GROUPS, lambda k: rest_copy(k).wait_send())
    loop(1, GROUPS, lambda k: plane_copy(k).wait_send())
    for k in range(1, 4):
        rest_line_copy(k).wait_send()
    rest_win.wait()
    loop(1, 8, lambda i: win_copy(i).wait())
    for layer in range(2):
        for block in range(5):
            vision_out[layer, :, block * COLS : (block + 1) * COLS] = windows[layer, block]


def scatter(text, vision):
    rows = text.shape[0]
    block = (GROUPS, ROWS, COLS)
    dma = pltpu.SemaphoreType.DMA
    return pl.pallas_call(
        scatter_kernel,
        name="sum_gradients",
        out_shape=(jax.ShapeDtypeStruct((rows, COLS), F32), jax.ShapeDtypeStruct((2, 24, 5 * COLS), F32)),
        in_specs=[pl.BlockSpec(memory_space=pltpu.HBM)] * 2,
        out_specs=[pl.BlockSpec(memory_space=pltpu.VMEM)] * 2,
        scratch_shapes=[
            pltpu.VMEM((5,) + block, BF16),
            pltpu.VMEM((5,) + block, BF16),
            pltpu.VMEM((5,) + block, BF16),
            pltpu.VMEM((8, ROWS, COLS), BF16),
            pltpu.VMEM((8, ROWS, COLS), BF16),
            pltpu.VMEM(block, BF16),
            pltpu.VMEM(block, BF16),
            pltpu.VMEM(block, BF16),
            pltpu.VMEM(block, BF16),
            pltpu.VMEM(block, BF16),
            pltpu.VMEM((ROWS, COLS), BF16),
            pltpu.VMEM((4, ROWS, COLS), BF16),
            pltpu.VMEM((ROWS, COLS), F32),
            pltpu.VMEM((ROWS, COLS), F32),
            pltpu.VMEM((2, 5, 24, COLS), F32),
            pltpu.VMEM((rows, COLS), BF16),
            pltpu.VMEM((8, rows, COLS), BF16),
            dma((5, 2)),
            dma,
            dma((5,)), dma((5,)),
            dma((6,)), dma((6,)),
            dma((GROUPS,)), dma((GROUPS,)),
            dma((GROUPS,)), dma((GROUPS,)),
            dma((4,)), dma((4,)),
            dma((8,)), dma((8,)),
            dma((8,)), dma((8,)),
        ],
        compiler_params=pltpu.CompilerParams(collective_id=1, has_side_effects=True, vmem_limit_bytes=40 << 20),
    )(text, vision)


def gather_kernel(
    text_w, vision_w, text_out, vision_out,
    staged, line_in, packed, blocks, from_pair,
    line_s, line_r, plane_s, plane_r, rest_s, rest_r, y_s, y_r, pair_s, pair_r, text_s, text_r, own_sem, out_sem,
):
    x, y, z, core = place()
    dp = x * 2 + z % 2
    group = group_of(x, z)
    cols_of = [(y + 2) % 4, (y + 1) % 4, (y + 3) % 4, 4, y]

    for layer in range(2):
        for block in range(4):
            staged[layer, block, :, :COLS] = vision_w[layer, :, block * COLS : (block + 1) * COLS]
            staged[layer, block, :, COLS:] = vision_w[layer, :, 4 * COLS :]

    greet(x, y, z, core)

    def line_copy(i):
        py, pc = line_partner(y, core, i)
        return remote(
            staged.at[pc, py], line_in.at[y * 2 + core], line_s.at[i], line_r.at[i], device(x, py, z, pc)
        )

    loop(1, 8, lambda i: line_copy(i).start())
    line_in[y * 2 + core] = staged[core, y]

    loop(1, 8, lambda i: line_copy(i).wait_recv())
    for i in range(8):
        packed[10 * i : 10 * i + 10, :] = line_in[i].astype(F32)[:10]
    blocks[OWN, group] = packed[:, :COLS].astype(BF16)
    blocks[REST, group] = packed[:, COLS:].astype(BF16)

    def plane_copy(k):
        px, pz = plane_partner(x, z, k)
        return remote(
            blocks.at[OWN, group], blocks.at[OWN, group], plane_s.at[k], plane_r.at[k], device(px, y, pz, core)
        )

    def rest_copy(k):
        px, pz = plane_partner(x, z, k)
        return remote(
            blocks.at[REST, group], blocks.at[REST, group], rest_s.at[k], rest_r.at[k], device(px, y, pz, core)
        )

    def text_cols(k):
        return text_out.at[:, pl.ds(pl.multiple_of(k * COLS, COLS), COLS)]

    def text_copy(k):
        return remote(text_w, text_cols(dp), text_s.at[k], text_r.at[k], ((dp + k) % 8, lax.axis_index("tensor")))

    loop(1, GROUPS, lambda k: plane_copy(k).start())
    own_text = pltpu.make_async_copy(text_w, text_cols(dp), own_sem)
    own_text.start()
    loop(1, 8, lambda k: text_copy(k).start())
    loop(1, GROUPS, lambda k: rest_copy(k).start())

    def pair(role):
        return remote(blocks.at[role], from_pair.at[role], pair_s.at[role], pair_r.at[role], device(x, y, z, 1 - core))

    def writes(role):
        cols = pl.ds(pl.multiple_of(cols_of[role] * COLS, COLS), COLS)
        return (
            pltpu.make_async_copy(blocks.at[role], vision_out.at[core, :, :, cols], out_sem.at[role, 0]),
            pltpu.make_async_copy(from_pair.at[role], vision_out.at[1 - core, :, :, cols], out_sem.at[role, 1]),
        )

    right, left = device(x, (y + 1) % 4, z, core), device(x, (y + 3) % 4, z, core)
    half_a, half_b = pl.ds(0, 8), pl.ds(8, 8)
    along = [
        remote(blocks.at[OWN, half_a], blocks.at[LEFT, half_a], y_s.at[0], y_r.at[0], right),
        remote(blocks.at[OWN, half_b], blocks.at[RIGHT, half_b], y_s.at[1], y_r.at[1], left),
        remote(blocks.at[OWN, half_b], blocks.at[LEFT, half_b], y_s.at[2], y_r.at[2], right),
        remote(blocks.at[OWN, half_a], blocks.at[RIGHT, half_a], y_s.at[3], y_r.at[3], left),
        remote(blocks.at[LEFT, half_a], blocks.at[OPP, half_a], y_s.at[4], y_r.at[4], right),
        remote(blocks.at[RIGHT, half_b], blocks.at[OPP, half_b], y_s.at[5], y_r.at[5], left),
    ]

    loop(1, GROUPS, lambda k: plane_copy(k).wait_recv())
    for copy in along[:4]:
        copy.start()
    pair(OWN).start()
    writes(OWN)[0].start()
    along[0].wait_recv()
    along[4].start()
    along[1].wait_recv()
    along[5].start()
    along[2].wait_recv()
    pair(LEFT).start()
    writes(LEFT)[0].start()
    along[3].wait_recv()
    pair(RIGHT).start()
    writes(RIGHT)[0].start()
    pair(OWN).wait_recv()
    writes(OWN)[1].start()
    loop(1, GROUPS, lambda k: rest_copy(k).wait_recv())
    pair(REST).start()
    writes(REST)[0].start()
    along[4].wait_recv()
    along[5].wait_recv()
    pair(OPP).start()
    writes(OPP)[0].start()
    for role in (LEFT, RIGHT, REST, OPP):
        pair(role).wait_recv()
        writes(role)[1].start()

    loop(1, 8, lambda i: line_copy(i).wait_send())
    loop(1, GROUPS, lambda k: plane_copy(k).wait_send())
    loop(1, GROUPS, lambda k: rest_copy(k).wait_send())
    own_text.wait()
    loop(1, 8, lambda k: text_copy(k).wait())
    for copy in along:
        copy.wait_send()
    for role in (OWN, LEFT, RIGHT, REST, OPP):
        pair(role).wait_send()
        for copy in writes(role):
            copy.wait()


def gather(text_w, vision_w):
    rows = text_w.shape[0]
    block = (GROUPS, ROWS, COLS)
    dma = pltpu.SemaphoreType.DMA
    return pl.pallas_call(
        gather_kernel,
        name="gather_weights",
        out_shape=(
            jax.ShapeDtypeStruct((rows, 8 * COLS), BF16),
            jax.ShapeDtypeStruct((2, GROUPS, ROWS, 5 * COLS), BF16),
        ),
        in_specs=[pl.BlockSpec(memory_space=pltpu.VMEM)] * 2,
        out_specs=[pl.BlockSpec(memory_space=pltpu.HBM)] * 2,
        scratch_shapes=[
            pltpu.VMEM((2, 4, 16, 2 * COLS), BF16),
            pltpu.VMEM((8, 16, 2 * COLS), BF16),
            pltpu.VMEM((ROWS, 2 * COLS), F32),
            pltpu.VMEM((5,) + block, BF16),
            pltpu.VMEM((5,) + block, BF16),
            dma((8,)), dma((8,)),
            dma((GROUPS,)), dma((GROUPS,)),
            dma((GROUPS,)), dma((GROUPS,)),
            dma((6,)), dma((6,)),
            dma((5,)), dma((5,)),
            dma((8,)), dma((8,)),
            dma,
            dma((5, 2)),
        ],
        compiler_params=pltpu.CompilerParams(collective_id=2, has_side_effects=True, vmem_limit_bytes=40 << 20),
    )(text_w, vision_w)


def body(
    text_grads, text_master, text_moment, text_second, text_ref,
    vision_grads, vision_master, vision_moment, vision_second, vision_ref,
):
    layers, width = vision_grads.shape[1], vision_grads.shape[3]
    text_total, windows = scatter(text_grads[0], vision_grads.reshape(layers, GROUPS, ROWS, width))
    _, y, _, core = place()
    first = 20 * y + 10 * core - 8 * ((5 * y) // 2)
    vision_total = lax.dynamic_slice_in_dim(windows, first, 10, axis=1)
    text_out = adam_step(text_total, text_moment, text_second, text_master, text_ref)
    vision_out = adam_step(vision_total, vision_moment, vision_second, vision_master, vision_ref)
    vision_padded = jnp.pad(vision_out[4], ((0, 0), (0, 6), (0, 0)))
    text_full, vision_full = gather(text_out[4], vision_padded)
    return text_out[:4] + (text_full,) + vision_out[:4] + (vision_full.reshape(layers, width, width),)


def solution(mesh):
    owned = P("tensor", "dp")
    vision_owned = P(None, ("dp", "tensor"), None)
    return jax.shard_map(
        body,
        mesh=mesh,
        in_specs=(P("dp", "tensor", None),) + (owned,) * 4 + (P(("dp", "tensor"), None, None, None),) + (vision_owned,) * 4,
        out_specs=(owned,) * 4 + (P("tensor", None),) + (vision_owned,) * 4 + (P(),),
        check_vma=False,
    )
```

time: 460 us -> 139 us (0.30)
  waiting for transfers between devices: 402 us -> 0 us
  Pallas kernels: 0 us -> 124 us
  other arithmetic: 34.4 us -> 2.45 us
  between operations: 15.3 us -> 0.86 us
    all_gather x2 -> x0, waiting for transfers between devices: 198 us -> none  [the longest x1 198 us: body(): lax.all_gather(vision_out[4], ('dp', 'tensor'), axis=1, tiled=True)]
    unnamed x5 -> x0, waiting for transfers between devices: 172 us -> none
    pallas_call x0 -> x2, Pallas kernels: none -> 124 us  [the longest x1 63.5 us: gather(): pl.pallas_call(gather_kernel, name='gather_weights', out_shape=(jax.Shape...]
    reduce_scatter x1 -> x0, waiting for transfers between devices: 31.6 us -> none  [body(): lax.psum_scatter(text_grads[0].astype(jnp.float32).astype(jnp.bfloat16),...]
    convert_element_type x3 -> x2, other arithmetic: 32.8 us -> 1.39 us  [adam_step(): master_new.astype(BF16)]
    unnamed x24 -> x28, local copies, waits for them, and re-layouts: 7.85 us -> 11.5 us
  transfers between devices with their start and end apart: 4 -> 0, of which waited for: 3 -> 0; matrix products, arithmetic and copies ran while one was open for 7% -> 0% of each run, Pallas kernels for 0% -> 0%
where the time goes in v1:
time: 139 us
  Pallas kernels  124 us (89%)
  local copies, waits for them, and re-layouts  11.5 us (8%)
  other arithmetic  2.45 us (2%)
    pallas_call x1, Pallas kernels, gather(): pl.pallas_call(gather_kernel, name='gather_weights', out_shape=(jax.Shape...  63.5 us
    pallas_call x1, Pallas kernels, scatter(): pl.pallas_call(scatter_kernel, name='sum_gradients', out_shape=(jax.Shape...  60.9 us
    unnamed x28, local copies, waits for them, and re-layouts  11.5 us

profile of v1, /device:TPU:1, one launch (start us, length us, event | category | flops | bytes accessed | tf_op | source)
XLA Modules:
  0.0 139.1 jit_solution(12391475861493065711)
XLA Ops:
  0.6 0.0 copy-start.7
  0.7 0.0 copy-start
  0.7 2.9 %copy-done = bf16[1,2,1280,1280]{3,2,1,0:T(8,128)(2,1)S(1)} copy-done((bf16[1,2,1280,1280]{3,2,1,0:T(8,128)(2,1)S(1)}, bf16[1,2,1280,1280]{3,2,1,0:T(8,128)(2,1)}, u32[]{:S(2)}) %copy-start) | copy-done | bytes 6553624
  3.6 0.0 copy-start.1
  3.6 1.6 %copy-done.1 = bf16[1,512,2048]{2,1,0:T(8,128)(2,1)S(1)} copy-done((bf16[1,512,2048]{2,1,0:T(8,128)(2,1)S(1)}, bf16[1,512,2048]{2,1,0:T(8,128)(2,1)}, u32[]{:S(2)}) %copy-start.1) | copy-done | bytes 2097176
  5.2 0.0 copy-start.8
  5.2 0.0 copy-start.9
  5.2 0.0 copy-start.10
  5.2 0.0 copy-start.3
  5.2 0.0 copy-start.4
  5.2 0.0 copy-start.5
  5.2 0.0 copy-start.6
  5.2 60.9 %sum_gradients.1 = (f32[512,256]{1,0:T(8,128)S(1)}, f32[2,24,1280]{2,1,0:T(8,128)S(1)}) custom-call(bf16[512,2048]{1,0:T(8,128)(2,1)S(1)} %bitcast.5, bf16[2,16,80,1280]{3,2,1,0:T(8,128)(2,1)S(1)} %bitcast.3), custom_call_target="tpu_custom_call" | custom-call | tf_op jit(solution)/shard_map/sum_gradients/pallas_call | solution.py:281
  66.1 0.0 copy-done.7
  66.1 0.0 copy-done.8
  66.1 0.0 copy-done.9
  66.1 0.0 copy-done.10
  66.2 0.2 fusion.4
  66.4 0.0 copy-done.3
  66.4 0.0 copy-done.4
  66.4 0.0 copy-done.5
  66.4 1.4 fusion.8
  67.8 63.5 %gather_weights.1 = (bf16[512,2048]{1,0:T(8,128)(2,1)S(1)}, bf16[2,16,80,1280]{3,2,1,0:T(8,128)(2,1)S(1)}) custom-call(bf16[512,256]{1,0:T(8,128)(2,1)S(1)} %get-tuple-element.32.text_w, bf16[2,16,1280]{2,1,0:T(8,128)(2,1)S(1)} %pad.4.vision_w), custom_call_target="tpu_custom_call" | custom-call | tf_op jit(solution)/shard_map/gather_weights/pallas_call | solution.py:441
  131.3 0.7 copy.25
  132.0 0.7 copy.26
  132.7 0.7 copy.27
  133.4 0.7 copy.28
  134.1 0.0 copy-done.6
  134.1 0.9 multiply_add_fusion
  135.0 1.3 copy.51
  136.3 2.8 %copy.52 = bf16[2,1280,1280]{2,1,0:T(8,128)(2,1)} copy(bf16[2,1280,1280]{2,1,0:T(8,128)(2,1)S(1)} %bitcast.4) | data formatting | bytes 13107200
  139.1 0.0 copy-done.2
  (3 shorter events, 0.0 us)
Async XLA Ops:
  0.6 65.5 %copy-start.7 = (f32[2,10,1280]{2,0,1:T(2,128)S(1)}, f32[2,10,1280]{2,0,1:T(2,128)}, u32[]{:S(2)}) copy-start(f32[2,10,1280]{2,0,1:T(2,128)} %param.19) | copy-start | bytes 307204
  0.7 2.9 %copy-start = (bf16[1,2,1280,1280]{3,2,1,0:T(8,128)(2,1)S(1)}, bf16[1,2,1280,1280]{3,2,1,0:T(8,128)(2,1)}, u32[]{:S(2)}) copy-start(bf16[1,2,1280,1280]{3,2,1,0:T(8,128)(2,1)} %param.15) | copy-start | bytes 19660804
  3.6 1.6 %copy-start.1 = (bf16[1,512,2048]{2,1,0:T(8,128)(2,1)S(1)}, bf16[1,512,2048]{2,1,0:T(8,128)(2,1)}, u32[]{:S(2)}) copy-start(bf16[1,512,2048]{2,1,0:T(8,128)(2,1)} %param.10) | copy-start | bytes 6291460
  5.2 60.9 %copy-start.8 = (f32[2,10,1280]{2,0,1:T(2,128)S(1)}, f32[2,10,1280]{2,0,1:T(2,128)}, u32[]{:S(2)}) copy-start(f32[2,10,1280]{2,0,1:T(2,128)} %param.16) | copy-start | bytes 307204
  5.2 61.0 %copy-start.9 = (f32[2,10,1280]{2,0,1:T(2,128)S(1)}, f32[2,10,1280]{2,0,1:T(2,128)}, u32[]{:S(2)}) copy-start(f32[2,10,1280]{2,0,1:T(2,128)} %param.17) | copy-start | bytes 307204
  5.2 61.0 %copy-start.10 = (f32[2,10,1280]{2,0,1:T(2,128)S(1)}, f32[2,10,1280]{2,0,1:T(2,128)}, u32[]{:S(2)}) copy-start(f32[2,10,1280]{2,0,1:T(2,128)} %param.18) | copy-start | bytes 307204
  5.2 61.2 %copy-start.3 = (f32[512,256]{1,0:T(8,128)S(1)}, f32[512,256]{1,0:T(8,128)}, u32[]{:S(2)}) copy-start(f32[512,256]{1,0:T(8,128)} %param.11) | copy-start | bytes 1572868
  5.2 61.2 %copy-start.4 = (f32[512,256]{1,0:T(8,128)S(1)}, f32[512,256]{1,0:T(8,128)}, u32[]{:S(2)}) copy-start(f32[512,256]{1,0:T(8,128)} %param.12) | copy-start | bytes 1572868
  5.2 61.2 %copy-start.5 = (f32[512,256]{1,0:T(8,128)S(1)}, f32[512,256]{1,0:T(8,128)}, u32[]{:S(2)}) copy-start(f32[512,256]{1,0:T(8,128)} %param.13) | copy-start | bytes 1572868
  5.2 128.9 %copy-start.6 = (f32[512,256]{1,0:T(8,128)S(1)}, f32[512,256]{1,0:T(8,128)}, u32[]{:S(2)}) copy-start(f32[512,256]{1,0:T(8,128)} %param.14) | copy-start | bytes 1572868
  67.8 71.4 %copy-start.2 = (f32[512,256]{1,0:T(8,128)}, f32[512,256]{1,0:T(8,128)S(1)}, u32[]{:S(2)}) copy-start(f32[512,256]{1,0:T(8,128)S(1)} %get-tuple-element.46) | copy-start | bytes 1572868

commit v2 on v0

v2 whole, which is shorter than its diff:
```python
import functools

import jax
import jax.numpy as jnp
from jax import lax
from jax.experimental import pallas as pl
from jax.experimental.pallas import tpu as pltpu
from jax.sharding import PartitionSpec as P

MESH = pl.DeviceIdType.MESH
BF16, F32 = jnp.bfloat16, jnp.float32

beta_one = 0.9
beta_two = 0.95
correct_one = 1.0 - 0.9**10
correct_two = 1.0 - 0.95**10
learn_rate = 0.01
decay_rate = 0.1
blend_rate = 0.6

GROUPS = 16
ROWS = 80
TILE = 128
COLS = 2 * TILE
OPP, RIGHT, LEFT, OWN, REST = range(5)
REST_0, REST_1, MAIN_0, MAIN_1 = range(4)


def adam_step(grad, moment, second, master, refcopy):
    moment_new = beta_one * moment + (1.0 - beta_one) * grad
    second_new = beta_two * second + (1.0 - beta_two) * grad * grad
    update = moment_new / correct_one / (jnp.sqrt(second_new / correct_two) + 1e-08)
    master_new = master - learn_rate * (update + decay_rate * master)
    ref_new = blend_rate * master_new + (1.0 - blend_rate) * refcopy
    return (master_new, moment_new, second_new, ref_new, master_new.astype(BF16))


def place():
    dp, tensor = lax.axis_index("dp"), lax.axis_index("tensor")
    x = dp // 2
    z = (tensor // 8) * 2 + dp % 2
    y = (tensor % 8) // 2
    return x, y, z, tensor % 2


def device(x, y, z, core):
    return (x * 2 + z % 2, (z // 2) * 8 + y * 2 + core)


def group_of(x, z):
    return x * 4 + (z % 2) * 2 + z // 2


def first_row(y):
    return pl.multiple_of(8 * ((5 * y) // 2), 8)


def columns(block, width):
    return pl.ds(pl.multiple_of(block * width, width), width)


def remote(src, dst, send, recv, to):
    return pltpu.make_async_remote_copy(
        src_ref=src, dst_ref=dst, send_sem=send, recv_sem=recv, device_id=to, device_id_type=MESH
    )


def loop(first, last, step):
    def run(i, carry):
        step(i)
        return carry

    lax.fori_loop(first, last, run, 0)


class Near:
    def __init__(self):
        self.x, self.y, self.z, self.core = place()
        x, y, z, core = self.x, self.y, self.z, self.core
        self.dp = x * 2 + z % 2
        self.twin = z % 2
        self.a = x * (1 - core) + z * core
        self.b = x * core + z * (1 - core)
        self.right = device(x, (y + 1) % 4, z, core)
        self.left = device(x, (y + 3) % 4, z, core)
        self.mate = device(x, y, z, 1 - core)
        self.beside = device(x, y, z + 1 - 2 * (z % 2), core)

    def along_a(self, k):
        core = self.core
        return device((self.x + k * (1 - core)) % 4, self.y, (self.z + k * core) % 4, core)

    def along_b(self, k):
        core = self.core
        return device((self.x + k * core) % 4, self.y, (self.z + k * (1 - core)) % 4, core)

    def along_x(self, k):
        return device((self.x + k) % 4, self.y, self.z, self.core)

    def line(self, i):
        py, pc = (self.y + i // 2) % 4, (self.core + i % 2) % 2
        return device(self.x, py, self.z, pc), py, pc

    def group(self, a, b):
        core = self.core
        return group_of(a * (1 - core) + b * core, a * core + b * (1 - core))

    def greet(self):
        barrier = pltpu.get_barrier_semaphore()

        def signal(to):
            pl.semaphore_signal(barrier, inc=1, device_id=to, device_id_type=MESH)

        loop(1, 4, lambda k: signal(self.along_a(k)))
        loop(1, 4, lambda k: signal(self.along_b(k)))
        loop(1, 8, lambda i: signal(self.line(i)[0]))
        pl.semaphore_wait(barrier, 13)


def scatter_kernel(
    text_hbm, vision_hbm, text_out, vision_out,
    mine, other, paired, main, rest, over_a, over_b, from_left, from_right, total, first_in, first_sum, second_in,
    rest_part, rest_line, sums, rest_sums, windows, upper, lower_own, lower_in, lower_sum, cross_out, cross_in, lower_x,
    load_sem, text_load, pair_s, pair_r, y_s, y_r, first_s, first_r, second_s, second_r, rest_y_s, rest_y_r,
    win_s, win_r, text_s, text_r, text2_s, text2_r,
):
    near = Near()
    x, y, core = near.x, near.y, near.core
    half_rows = text_hbm.shape[0] // 2
    blocks = [(y + 2) % 4, (y + 1) % 4, (y + 3) % 4, y, 4]
    order = (OPP, RIGHT, LEFT, REST, OWN)

    def loads(role):
        cols = columns(blocks[role], COLS)
        return (
            pltpu.make_async_copy(vision_hbm.at[1 - core, :, :, cols], other.at[role], load_sem.at[role, 0]),
            pltpu.make_async_copy(vision_hbm.at[core, :, :, cols], mine.at[role], load_sem.at[role, 1]),
        )

    def text_block(half, block):
        return text_hbm.at[pl.ds(half * half_rows, half_rows), columns(block, COLS)]

    def upper_load(q):
        return pltpu.make_async_copy(text_block(0, 2 * x + q), upper.at[0, q], text_load.at[q])

    def lower_load(px):
        return pltpu.make_async_copy(text_block(1, 2 * px + near.twin), lower_own.at[px], text_load.at[2 + px])

    for role in order:
        for copy in loads(role):
            copy.start()
    loop(0, 2, lambda q: upper_load(q).start())
    loop(0, 4, lambda px: lower_load(px).start())

    near.greet()

    def upper_copy(k, q):
        to = (x + k) % 4
        return remote(
            text_block(0, 2 * to + q), upper.at[k, q], text_s.at[k, q], text_r.at[k, q], near.along_x(k)
        )

    def lower_copy(px):
        return remote(
            text_block(1, 2 * px + 1 - near.twin), lower_in.at[px], text_s.at[4 + px, 0], text_r.at[4 + px, 0],
            near.beside,
        )

    def pair(role):
        return remote(other.at[role], paired.at[role], pair_s.at[role], pair_r.at[role], near.mate)

    for role in order:
        loads(role)[0].wait()
        pair(role).start()

    for k in range(1, 4):
        for q in range(2):
            upper_copy(k, q).start()
    loop(0, 4, lambda px: lower_copy(px).start())

    def ready(role):
        loads(role)[1].wait()
        pair(role).wait_recv()

    def add_pair(role):
        ready(role)

        def add(g):
            both = mine[role, g] + paired[role, g]
            main[role, 0, g] = both[:, :TILE]
            main[role, 1, g] = both[:, TILE:]

        loop(0, GROUPS, add)

    def add_rest():
        ready(REST)

        def add(i):
            a, b = i // 4, i % 4
            g = near.group(a, b)
            both = mine[REST, g] + paired[REST, g]
            rest[0, a, b] = both[:, :TILE]
            rest[1, a, b] = both[:, TILE:]

        loop(0, GROUPS, add)

    half_a, half_b = pl.ds(0, 8), pl.ds(8, 8)

    def along(tile):
        def go(src, dst, i, to):
            return remote(src, dst, y_s.at[tile, i], y_r.at[tile, i], to)

        return [
            go(main.at[OPP, tile, half_a], over_a.at[tile], 0, near.right),
            go(main.at[OPP, tile, half_b], over_b.at[tile], 1, near.left),
            go(main.at[RIGHT, tile, half_b], from_left.at[tile, half_b], 2, near.right),
            go(main.at[LEFT, tile, half_a], from_right.at[tile, half_a], 3, near.left),
            go(main.at[RIGHT, tile, half_a], from_left.at[tile, half_a], 4, near.right),
            go(main.at[LEFT, tile, half_b], from_right.at[tile, half_b], 5, near.left),
        ]

    line = [along(0), along(1)]

    def pass_on(tile):
        line[tile][0].wait_recv()

        def add_a(g):
            main[RIGHT, tile, g] = main[RIGHT, tile, g] + over_a[tile, g]

        loop(0, 8, add_a)
        line[tile][4].start()
        line[tile][1].wait_recv()

        def add_b(g):
            main[LEFT, tile, 8 + g] = main[LEFT, tile, 8 + g] + over_b[tile, g]

        loop(0, 8, add_b)
        line[tile][5].start()

    def add_line(tile):
        for copy in line[tile][2:]:
            copy.wait_recv()

        def add(i):
            a, b = i // 4, i % 4
            g = near.group(a, b)
            total[tile, a, b] = (
                main[OWN, tile, g].astype(F32) + from_left[tile, g].astype(F32) + from_right[tile, g].astype(F32)
            ).astype(BF16)

        loop(0, GROUPS, add)

    def source(part):
        return rest.at[part] if part < MAIN_0 else total.at[part - MAIN_0]

    def first_copy(part, k):
        return remote(
            source(part).at[(near.a + k) % 4], first_in.at[part, k], first_s.at[part, k], first_r.at[part, k],
            near.along_a(k),
        )

    def second_copy(part, k):
        return remote(
            first_sum.at[part, (near.b + k) % 4], second_in.at[part, k], second_s.at[part, k], second_r.at[part, k],
            near.along_b(k),
        )

    def first_step(part):
        loop(1, 4, lambda k: first_copy(part, k).start())

    def second_step(part):
        loop(1, 4, lambda k: first_copy(part, k).wait_recv())
        own = source(part).at[near.a]

        def add(b):
            acc = own[b].astype(F32)
            for k in range(1, 4):
                acc = acc + first_in[part, k, b].astype(F32)
            first_sum[part, b] = acc.astype(BF16)

        loop(0, 4, add)
        loop(1, 4, lambda k: second_copy(part, k).start())

    def last_step(part):
        loop(1, 4, lambda k: second_copy(part, k).wait_recv())
        acc = first_sum[part, near.b].astype(F32)
        for k in range(1, 4):
            acc = acc + second_in[part, k].astype(F32)
        return acc

    add_pair(OPP)
    line[0][0].start()
    line[0][1].start()
    add_pair(RIGHT)
    line[0][2].start()
    add_pair(LEFT)
    line[0][3].start()
    add_rest()
    first_step(REST_0)
    first_step(REST_1)
    add_pair(OWN)
    pass_on(0)
    for copy in line[1][:4]:
        copy.start()
    second_step(REST_0)
    second_step(REST_1)

    def cross_copy():
        return remote(cross_out, cross_in, text2_s.at[0], text2_r.at[0], near.beside)

    def lower_x_copy(k):
        return remote(
            lower_sum.at[(x + k) % 4], lower_x.at[k], text2_s.at[k], text2_r.at[k], near.along_x(k)
        )

    def text_middle():
        loop(0, 2, lambda q: upper_load(q).wait())
        for k in range(1, 4):
            for q in range(2):
                upper_copy(k, q).wait_recv()

        def add_upper(i):
            rows = pl.ds(pl.multiple_of(i * 32, 32), 32)
            acc_out = upper[0, 1 - near.twin, rows].astype(F32)
            acc_own = upper[0, near.twin, rows].astype(F32)
            for k in range(1, 4):
                acc_out = acc_out + upper[k, 1 - near.twin, rows].astype(F32)
                acc_own = acc_own + upper[k, near.twin, rows].astype(F32)
            cross_out[rows] = acc_out.astype(BF16)
            text_out[rows] = acc_own

        loop(0, half_rows // 32, add_upper)
        cross_copy().start()
        loop(0, 4, lambda px: lower_load(px).wait())
        loop(0, 4, lambda px: lower_copy(px).wait_recv())

        def add_lower(i):
            px, rows = i // 4, pl.ds(pl.multiple_of((i % 4) * 64, 64), 64)
            lower_sum[px, rows] = lower_own[px, rows] + lower_in[px, rows]

        loop(0, half_rows // 16, add_lower)
        loop(1, 4, lambda k: lower_x_copy(k).start())

    def text_last():
        cross_copy().wait_recv()
        loop(1, 4, lambda k: lower_x_copy(k).wait_recv())

        def add(i):
            rows = pl.ds(pl.multiple_of(i * 32, 32), 32)
            text_out[rows] = text_out[rows] + cross_in[rows].astype(F32)
            acc = lower_own[x, rows].astype(F32) + lower_in[x, rows].astype(F32)
            for k in range(1, 4):
                acc = acc + lower_x[k, rows].astype(F32)
            text_out[pl.ds(pl.multiple_of(half_rows + i * 32, 32), 32)] = acc

        loop(0, half_rows // 32, add)

    def rest_line_copy(k):
        return remote(
            rest_part, rest_line.at[k], rest_y_s.at[k], rest_y_r.at[k], device(x, (y + k) % 4, near.z, core)
        )

    own_rows = pl.ds(first_row(y), 24)

    def rest_win():
        return remote(
            rest_sums.at[:, own_rows], windows.at[core, pl.ds(8, 2)], win_s.at[0, 0], win_r.at[0, 0], near.mate
        )

    def win_copy(tile, i):
        to, py, _ = near.line(i)
        return remote(
            sums.at[tile, pl.ds(first_row(py), 24)], windows.at[core, 2 * y + tile], win_s.at[tile, i], win_r.at[tile, i],
            to,
        )

    def main_last(tile):
        sums[tile] = last_step(MAIN_0 + tile)
        loop(1, 8, lambda i: win_copy(tile, i).start())
        windows[core, 2 * y + tile] = sums[tile, own_rows]

    add_line(0)
    first_step(MAIN_0)
    pass_on(1)
    text_middle()
    for tile in range(2):
        rest_part[tile] = last_step(REST_0 + tile).astype(BF16)
    loop(1, 4, lambda k: rest_line_copy(k).start())
    second_step(MAIN_0)
    add_line(1)
    first_step(MAIN_1)

    loop(1, 4, lambda k: rest_line_copy(k).wait_recv())
    for tile in range(2):
        acc = rest_part[tile].astype(F32)
        for k in range(1, 4):
            acc = acc + rest_line[k, tile].astype(F32)
        rest_sums[tile] = acc
        windows[core, 8 + tile] = rest_sums[tile, own_rows]
    rest_win().start()
    main_last(0)
    second_step(MAIN_1)
    text_last()
    main_last(1)

    for role in order:
        pair(role).wait_send()
    for copy in line[0] + line[1]:
        copy.wait_send()
    for k in range(1, 4):
        for q in range(2):
            upper_copy(k, q).wait_send()
    loop(0, 4, lambda px: lower_copy(px).wait_send())
    cross_copy().wait_send()
    loop(1, 4, lambda k: lower_x_copy(k).wait_send())
    for part in range(4):
        loop(1, 4, lambda k: first_copy(part, k).wait_send())
        loop(1, 4, lambda k: second_copy(part, k).wait_send())
    loop(1, 4, lambda k: rest_line_copy(k).wait_send())
    rest_win().wait()
    for tile in range(2):
        loop(1, 8, lambda i: win_copy(tile, i).wait())
    for layer in range(2):
        for t in range(10):
            vision_out[layer, :, t * TILE : (t + 1) * TILE] = windows[layer, t]


def scatter(text, vision):
    rows = text.shape[0]
    half = rows // 2
    block = (GROUPS, ROWS, COLS)
    tile = (GROUPS, ROWS, TILE)
    plane = (4, 4, ROWS, TILE)
    dma = pltpu.SemaphoreType.DMA
    return pl.pallas_call(
        scatter_kernel,
        name="sum_gradients",
        out_shape=(jax.ShapeDtypeStruct((rows, COLS), F32), jax.ShapeDtypeStruct((2, 24, 5 * COLS), F32)),
        in_specs=[pl.BlockSpec(memory_space=pltpu.HBM)] * 2,
        out_specs=[pl.BlockSpec(memory_space=pltpu.VMEM)] * 2,
        scratch_shapes=[
            pltpu.VMEM((5,) + block, BF16),
            pltpu.VMEM((5,) + block, BF16),
            pltpu.VMEM((5,) + block, BF16),
            pltpu.VMEM((4, 2) + tile, BF16),
            pltpu.VMEM((2,) + plane, BF16),
            pltpu.VMEM((2, 8, ROWS, TILE), BF16),
            pltpu.VMEM((2, 8, ROWS, TILE), BF16),
            pltpu.VMEM((2,) + tile, BF16),
            pltpu.VMEM((2,) + tile, BF16),
            pltpu.VMEM((2,) + plane, BF16),
            pltpu.VMEM((4,) + plane, BF16),
            pltpu.VMEM((4, 4, ROWS, TILE), BF16),
            pltpu.VMEM((4, 4, ROWS, TILE), BF16),
            pltpu.VMEM((2, ROWS, TILE), BF16),
            pltpu.VMEM((4, 2, ROWS, TILE), BF16),
            pltpu.VMEM((2, ROWS, TILE), F32),
            pltpu.VMEM((2, ROWS, TILE), F32),
            pltpu.VMEM((2, 10, 24, TILE), F32),
            pltpu.VMEM((4, 2, half, COLS), BF16),
            pltpu.VMEM((4, half, COLS), BF16),
            pltpu.VMEM((4, half, COLS), BF16),
            pltpu.VMEM((4, half, COLS), BF16),
            pltpu.VMEM((half, COLS), BF16),
            pltpu.VMEM((half, COLS), BF16),
            pltpu.VMEM((4, half, COLS), BF16),
            dma((5, 2)),
            dma((6,)),
            dma((5,)), dma((5,)),
            dma((2, 6)), dma((2, 6)),
            dma((4, 4)), dma((4, 4)),
            dma((4, 4)), dma((4, 4)),
            dma((4,)), dma((4,)),
            dma((2, 8)), dma((2, 8)),
            dma((8, 2)), dma((8, 2)),
            dma((4,)), dma((4,)),
        ],
        compiler_params=pltpu.CompilerParams(collective_id=1, has_side_effects=True, vmem_limit_bytes=SCATTER_VMEM),
    )(text, vision)


SCATTER_VMEM = 56 << 20


def gather_kernel(
    text_w, vision_w, text_out, vision_out,
    staged, line_in, packed, plane, main, rest, from_pair,
    line_s, line_r, first_s, first_r, second_s, second_r, y_s, y_r, pair_s, pair_r, text_s, text_r, own_sem, out_sem,
):
    near = Near()
    x, y, core = near.x, near.y, near.core
    half_rows = text_w.shape[0] // 2
    upper, lower = pl.ds(0, half_rows), pl.ds(half_rows, half_rows)

    for layer in range(2):
        for block in range(4):
            staged[layer, block, :, :COLS] = vision_w[layer, :, block * COLS : (block + 1) * COLS]
            staged[layer, block, :, COLS:] = vision_w[layer, :, 4 * COLS :]

    near.greet()

    def line_copy(i):
        to, py, pc = near.line(i)
        return remote(staged.at[pc, py], line_in.at[y * 2 + core], line_s.at[i], line_r.at[i], to)

    own_cols = columns(near.dp, COLS)

    def own_text():
        return pltpu.make_async_copy(text_w, text_out.at[:, own_cols], own_sem)

    def beside_copy():
        return remote(text_w.at[upper], text_out.at[upper, own_cols], text_s.at[0, 0], text_r.at[0, 0], near.beside)

    def x_copy(k):
        return remote(text_w.at[lower], text_out.at[lower, own_cols], text_s.at[0, k], text_r.at[0, k], near.along_x(k))

    def upper_copy(k):
        both = text_out.at[upper, columns(x, 2 * COLS)]
        return remote(both, both, text_s.at[1, k], text_r.at[1, k], near.along_x(k))

    def lower_copy(px):
        one = text_out.at[lower, columns(2 * px + near.twin, COLS)]
        return remote(one, one, text_s.at[2, px], text_r.at[2, px], near.beside)

    loop(1, 8, lambda i: line_copy(i).start())
    own_text().start()
    beside_copy().start()
    loop(1, 4, lambda k: x_copy(k).start())
    line_in[y * 2 + core] = staged[core, y]
    loop(1, 8, lambda i: line_copy(i).wait_recv())
    for i in range(8):
        packed[10 * i : 10 * i + 10, :] = line_in[i].astype(F32)[:10]
    for part, first in ((MAIN_0, 0), (MAIN_1, 1), (REST_0, 2), (REST_1, 3)):
        plane[part, near.a, near.b] = packed[:, first * TILE : (first + 1) * TILE].astype(BF16)

    def first_copy(part, k):
        one = plane.at[part, near.a, near.b]
        return remote(one, one, first_s.at[part, k], first_r.at[part, k], near.along_b(k))

    def second_copy(part, k):
        row = plane.at[part, near.a]
        return remote(row, row, second_s.at[part, k], second_r.at[part, k], near.along_a(k))

    parts = (MAIN_0, MAIN_1, REST_0, REST_1)
    for part in parts:
        loop(1, 4, lambda k: first_copy(part, k).start())
    for part in parts:
        loop(1, 4, lambda k: first_copy(part, k).wait_recv())
        loop(1, 4, lambda k: second_copy(part, k).start())

    def spread(part, dst):
        loop(1, 4, lambda k: second_copy(part, k).wait_recv())

        def move(i):
            a, b = i // 4, i % 4
            dst[near.group(a, b)] = plane[part, a, b]

        loop(0, GROUPS, move)

    half_a, half_b = pl.ds(0, 8), pl.ds(8, 8)

    def along(tile):
        def go(src, dst, half, i, to):
            return remote(main.at[src, tile, half], main.at[dst, tile, half], y_s.at[tile, i], y_r.at[tile, i], to)

        return [
            go(OWN, LEFT, half_a, 0, near.right),
            go(OWN, RIGHT, half_b, 1, near.left),
            go(OWN, LEFT, half_b, 2, near.right),
            go(OWN, RIGHT, half_a, 3, near.left),
            go(LEFT, OPP, half_a, 4, near.right),
            go(RIGHT, OPP, half_b, 5, near.left),
        ]

    line = [along(0), along(1)]
    tiles = {OPP: 2 * ((y + 2) % 4), RIGHT: 2 * ((y + 1) % 4), LEFT: 2 * ((y + 3) % 4), OWN: 2 * y, REST: 8}

    def held(role, tile):
        return rest.at[tile] if role == REST else main.at[role, tile]

    def pair(role, tile):
        return remote(
            held(role, tile), from_pair.at[role, tile], pair_s.at[role, tile], pair_r.at[role, tile], near.mate
        )

    def write(role, tile, which):
        src = from_pair.at[role, tile] if which else held(role, tile)
        layer = 1 - core if which else core
        cols = columns(tiles[role] + tile, TILE)
        return pltpu.make_async_copy(src, vision_out.at[layer, :, :, cols], out_sem.at[role, tile, which])

    def give(role, tile):
        pair(role, tile).start()
        write(role, tile, 0).start()

    spread(MAIN_0, main.at[OWN, 0])
    for copy in line[0][:4]:
        copy.start()
    spread(MAIN_1, main.at[OWN, 1])
    give(OWN, 0)
    give(OWN, 1)

    own_text().wait()
    beside_copy().wait_recv()
    loop(1, 4, lambda k: upper_copy(k).start())
    loop(1, 4, lambda k: x_copy(k).wait_recv())
    loop(0, 4, lambda px: lower_copy(px).start())

    line[0][0].wait_recv()
    line[0][4].start()
    line[0][1].wait_recv()
    line[0][5].start()
    for copy in line[1][:4]:
        copy.start()

    for tile in range(2):
        spread(REST_0 + tile, rest.at[tile])
        give(REST, tile)
    for tile in range(2):
        line[tile][2].wait_recv()
        give(LEFT, tile)
        line[tile][3].wait_recv()
        give(RIGHT, tile)
        if tile == 0:
            line[1][0].wait_recv()
            line[1][4].start()
            line[1][1].wait_recv()
            line[1][5].start()
        line[tile][4].wait_recv()
        line[tile][5].wait_recv()
        give(OPP, tile)

    arrivals = [(OWN, 0), (OWN, 1), (REST, 0), (REST, 1), (LEFT, 0), (RIGHT, 0), (OPP, 0), (LEFT, 1), (RIGHT, 1), (OPP, 1)]
    loop(1, 8, lambda i: line_copy(i).wait_send())
    for part in parts:
        loop(1, 4, lambda k: first_copy(part, k).wait_send())
        loop(1, 4, lambda k: second_copy(part, k).wait_send())
    beside_copy().wait_send()
    loop(1, 4, lambda k: x_copy(k).wait_send())
    loop(1, 4, lambda k: upper_copy(k).wait())
    loop(0, 4, lambda px: lower_copy(px).wait())
    for role, tile in arrivals:
        pair(role, tile).wait_recv()
        write(role, tile, 1).start()
    for copy in line[0] + line[1]:
        copy.wait_send()
    for role, tile in arrivals:
        pair(role, tile).wait_send()
        write(role, tile, 0).wait()
        write(role, tile, 1).wait()


def gather(text_w, vision_w):
    rows = text_w.shape[0]
    tile = (GROUPS, ROWS, TILE)
    dma = pltpu.SemaphoreType.DMA
    return pl.pallas_call(
        gather_kernel,
        name="gather_weights",
        out_shape=(
            jax.ShapeDtypeStruct((rows, 8 * COLS), BF16),
            jax.ShapeDtypeStruct((2, GROUPS, ROWS, 5 * COLS), BF16),
        ),
        in_specs=[pl.BlockSpec(memory_space=pltpu.VMEM)] * 2,
        out_specs=[pl.BlockSpec(memory_space=pltpu.HBM)] * 2,
        scratch_shapes=[
            pltpu.VMEM((2, 4, 16, 2 * COLS), BF16),
            pltpu.VMEM((8, 16, 2 * COLS), BF16),
            pltpu.VMEM((ROWS, 2 * COLS), F32),
            pltpu.VMEM((4, 4, 4, ROWS, TILE), BF16),
            pltpu.VMEM((4, 2) + tile, BF16),
            pltpu.VMEM((2,) + tile, BF16),
            pltpu.VMEM((5, 2) + tile, BF16),
            dma((8,)), dma((8,)),
            dma((4, 4)), dma((4, 4)),
            dma((4, 4)), dma((4, 4)),
            dma((2, 6)), dma((2, 6)),
            dma((5, 2)), dma((5, 2)),
            dma((3, 4)), dma((3, 4)),
            dma,
            dma((5, 2, 2)),
        ],
        compiler_params=pltpu.CompilerParams(collective_id=2, has_side_effects=True, vmem_limit_bytes=24 << 20),
    )(text_w, vision_w)


def body(
    text_grads, text_master, text_moment, text_second, text_ref,
    vision_grads, vision_master, vision_moment, vision_second, vision_ref,
):
    layers, width = vision_grads.shape[1], vision_grads.shape[3]
    text_total, windows = scatter(text_grads[0], vision_grads.reshape(layers, GROUPS, ROWS, width))
    _, y, _, core = place()
    first = 20 * y + 10 * core - 8 * ((5 * y) // 2)
    vision_total = lax.dynamic_slice_in_dim(windows, first, 10, axis=1)
    text_out = adam_step(text_total, text_moment, text_second, text_master, text_ref)

    def rows_first(array):
        return jnp.transpose(array, (1, 0, 2))

    vision_out = adam_step(*map(rows_first, (vision_total, vision_moment, vision_second, vision_master, vision_ref)))
    vision_out = tuple(map(rows_first, vision_out))
    vision_padded = jnp.pad(vision_out[4], ((0, 0), (0, 6), (0, 0)))
    text_full, vision_full = gather(text_out[4], vision_padded)
    return text_out[:4] + (text_full,) + vision_out[:4] + (vision_full.reshape(layers, width, width),)


def solution(mesh):
    owned = P("tensor", "dp")
    vision_owned = P(None, ("dp", "tensor"), None)
    return jax.shard_map(
        body,
        mesh=mesh,
        in_specs=(P("dp", "tensor", None),) + (owned,) * 4 + (P(("dp", "tensor"), None, None, None),) + (vision_owned,) * 4,
        out_specs=(owned,) * 4 + (P("tensor", None),) + (vision_owned,) * 4 + (P(),),
        check_vma=False,
    )
```

time: 460 us -> 105 us (0.23)
  waiting for transfers between devices: 402 us -> 0 us
  Pallas kernels: 0 us -> 92.3 us
  other arithmetic: 34.4 us -> 4.41 us
  between operations: 15.3 us -> 0.87 us
    all_gather x2 -> x0, waiting for transfers between devices: 198 us -> none  [the longest x1 198 us: body(): lax.all_gather(vision_out[4], ('dp', 'tensor'), axis=1, tiled=True)]
    unnamed x5 -> x0, waiting for transfers between devices: 172 us -> none
    pallas_call x0 -> x2, Pallas kernels: none -> 92.3 us  [the longest x1 50.7 us: scatter(): pl.pallas_call(scatter_kernel, name='sum_gradients', out_shape=(jax.Shape...]
    reduce_scatter x1 -> x0, waiting for transfers between devices: 31.6 us -> none  [body(): lax.psum_scatter(text_grads[0].astype(jnp.float32).astype(jnp.bfloat16),...]
    convert_element_type x3 -> x2, other arithmetic: 32.8 us -> 2.43 us  [adam_step(): master_new.astype(BF16)]
  transfers between devices with their start and end apart: 4 -> 0, of which waited for: 3 -> 0; matrix products, arithmetic and copies ran while one was open for 7% -> 0% of each run, Pallas kernels for 0% -> 0%
where the time goes in v2:
time: 105 us
  Pallas kernels  92.3 us (88%)
  local copies, waits for them, and re-layouts  7.04 us (7%)
  other arithmetic  4.41 us (4%)
    pallas_call x1, Pallas kernels, scatter(): pl.pallas_call(scatter_kernel, name='sum_gradients', out_shape=(jax.Shape...  50.7 us
    pallas_call x1, Pallas kernels, gather(): pl.pallas_call(gather_kernel, name='gather_weights', out_shape=(jax.Shape...  41.5 us
    unnamed x24, local copies, waits for them, and re-layouts  7.03 us
    convert_element_type x2, other arithmetic, adam_step(): master_new.astype(BF16)  2.43 us

profile of v2, /device:TPU:1, one launch (start us, length us, event | category | flops | bytes accessed | tf_op | source)
XLA Modules:
  0.0 104.6 jit_solution(6420661588725298582)
XLA Ops:
  0.6 0.0 copy-start.6
  0.7 0.0 copy-start.7
  0.7 0.0 copy-start.8
  0.7 0.0 copy-start.5
  0.7 0.0 copy-start.1
  0.7 0.0 copy-start.2
  0.7 0.0 copy-start.3
  0.8 0.0 copy-start.4
  0.8 50.7 %sum_gradients.1 = (f32[512,256]{1,0:T(8,128)}, f32[2,24,1280]{2,1,0:T(8,128)}) custom-call(bf16[512,2048]{1,0:T(8,128)(2,1)} %bitcast.5, bf16[2,16,80,1280]{3,2,1,0:T(8,128)(2,1)} %bitcast.4), custom_call_target="tpu_custom_call" | custom-call | tf_op jit(solution)/shard_map/sum_gradients/pallas_call | solution.py:435
  51.5 0.0 copy-done.6
  51.5 0.0 copy-done.7
  51.5 0.0 copy-done.8
  51.5 0.0 copy-done.5
  51.6 1.1 %fusion.4 = (f32[2,10,1280]{2,1,0:T(8,128)S(1)}, f32[2,10,1280]{2,1,0:T(8,128)S(1)}, f32[2,10,1280]{2,1,0:T(8,128)S(1)}, f32[2,10,1280]{2,1,0:T(8,128)S(1)}) fusion(f32[2,10,1280]{2,0,1:T(2,128)S(1)} %copy-done.5, f32[2,10,1280]{2,0,1:T(2,128)S(1)} %copy-done.6, f32[2,24,1280]{2,1,0:T(8,128)} %get-tuple-element.15, s32[]{:T(128)S(6)} %select_n.25, ...), kind=kLoop, calls=%fused_computation.12 | loop fusion | flops 460800 | bytes 921604 | tf_op jit(solution)/shard_map/add | solution.py:34
  52.7 0.0 copy-done.1
  52.7 0.0 copy-done.2
  52.7 0.0 copy-done.3
  52.7 2.4 %fusion.8 = (bf16[512,256]{1,0:T(8,128)(2,1)S(1)}, f32[512,256]{1,0:T(8,128)S(1)}, f32[512,256]{1,0:T(8,128)}, f32[512,256]{1,0:T(8,128)}) fusion(f32[512,256]{1,0:T(8,128)S(1)} %copy-done.1, f32[512,256]{1,0:T(8,128)} %get-tuple-element.14, f32[512,256]{1,0:T(8,128)S(1)} %copy-done.2, f32[512,256]{1,0:T(8,128)S(1)} %copy-done.3), kind=kLoop, calls=%fused_computation.16 | loop fusion | flops 2097152 | bytes 3932160 | tf_op jit(solution)/shard_map/convert_element_type | solution.py:35
  55.1 0.0 copy-start
  55.2 41.5 %gather_weights.1 = (bf16[512,2048]{1,0:T(8,128)(2,1)S(1)}, bf16[2,16,80,1280]{3,2,1,0:T(8,128)(2,1)S(1)}) custom-call(bf16[512,256]{1,0:T(8,128)(2,1)S(1)} %get-tuple-element.32.text_w, bf16[2,16,1280]{2,1,0:T(8,128)(2,1)S(1)} %pad.4.vision_w), custom_call_target="tpu_custom_call" | custom-call | tf_op jit(solution)/shard_map/gather_weights/pallas_call | solution.py:657
  96.7 0.7 copy.25
  97.4 0.7 copy.26
  98.2 0.7 copy.27
  98.9 0.7 copy.28
  99.6 0.0 copy-done.4
  99.6 0.9 multiply_add_fusion
  100.5 1.3 %copy.51 = bf16[512,2048]{1,0:T(8,128)(2,1)} copy(bf16[512,2048]{1,0:T(8,128)(2,1)S(1)} %get-tuple-element.50) | data formatting | bytes 4194304
  101.8 2.8 %copy.52 = bf16[2,1280,1280]{2,1,0:T(8,128)(2,1)} copy(bf16[2,1280,1280]{2,1,0:T(8,128)(2,1)S(1)} %bitcast.3) | data formatting | bytes 13107200
  104.6 0.0 copy-done
  (2 shorter events, 0.0 us)
Async XLA Ops:
  0.6 50.9 %copy-start.6 = (f32[2,10,1280]{2,0,1:T(2,128)S(1)}, f32[2,10,1280]{2,0,1:T(2,128)}, u32[]{:S(2)}) copy-start(f32[2,10,1280]{2,0,1:T(2,128)} %param.16) | copy-start | bytes 307204
  0.7 50.9 %copy-start.7 = (f32[2,10,1280]{2,0,1:T(2,128)S(1)}, f32[2,10,1280]{2,0,1:T(2,128)}, u32[]{:S(2)}) copy-start(f32[2,10,1280]{2,0,1:T(2,128)} %param.17) | copy-start | bytes 307204
  0.7 50.9 %copy-start.8 = (f32[2,10,1280]{2,0,1:T(2,128)S(1)}, f32[2,10,1280]{2,0,1:T(2,128)}, u32[]{:S(2)}) copy-start(f32[2,10,1280]{2,0,1:T(2,128)} %param.18) | copy-start | bytes 307204
  0.7 50.9 %copy-start.5 = (f32[2,10,1280]{2,0,1:T(2,128)S(1)}, f32[2,10,1280]{2,0,1:T(2,128)}, u32[]{:S(2)}) copy-start(f32[2,10,1280]{2,0,1:T(2,128)} %param.19) | copy-start | bytes 307204
  0.7 52.0 %copy-start.1 = (f32[512,256]{1,0:T(8,128)S(1)}, f32[512,256]{1,0:T(8,128)}, u32[]{:S(2)}) copy-start(f32[512,256]{1,0:T(8,128)} %param.11) | copy-start | bytes 1572868
  0.7 52.0 %copy-start.2 = (f32[512,256]{1,0:T(8,128)S(1)}, f32[512,256]{1,0:T(8,128)}, u32[]{:S(2)}) copy-start(f32[512,256]{1,0:T(8,128)} %param.12) | copy-start | bytes 1572868
  0.7 52.0 %copy-start.3 = (f32[512,256]{1,0:T(8,128)S(1)}, f32[512,256]{1,0:T(8,128)}, u32[]{:S(2)}) copy-start(f32[512,256]{1,0:T(8,128)} %param.13) | copy-start | bytes 1572868
  0.8 98.8 %copy-start.4 = (f32[512,256]{1,0:T(8,128)S(1)}, f32[512,256]{1,0:T(8,128)}, u32[]{:S(2)}) copy-start(f32[512,256]{1,0:T(8,128)} %param.14) | copy-start | bytes 1572868
  55.1 49.4 %copy-start = (f32[512,256]{1,0:T(8,128)}, f32[512,256]{1,0:T(8,128)S(1)}, u32[]{:S(2)}) copy-start(f32[512,256]{1,0:T(8,128)S(1)} %get-tuple-element.46) | copy-start | bytes 1572868

commit v3 on v2

v3 whole, which is shorter than its diff:
```python
import functools

import jax
import jax.numpy as jnp
from jax import lax
from jax.experimental import pallas as pl
from jax.experimental.pallas import tpu as pltpu
from jax.sharding import PartitionSpec as P

MESH = pl.DeviceIdType.MESH
BF16, F32 = jnp.bfloat16, jnp.float32

beta_one = 0.9
beta_two = 0.95
correct_one = 1.0 - 0.9**10
correct_two = 1.0 - 0.95**10
learn_rate = 0.01
decay_rate = 0.1
blend_rate = 0.6

GROUPS = 16
ROWS = 80
TILE = 128
COLS = 2 * TILE
OPP, RIGHT, LEFT, OWN, REST = range(5)
REST_0, REST_1, MAIN_0, MAIN_1 = range(4)


def adam_step(grad, moment, second, master, refcopy):
    moment_new = beta_one * moment + (1.0 - beta_one) * grad
    second_new = beta_two * second + (1.0 - beta_two) * grad * grad
    update = moment_new / correct_one / (jnp.sqrt(second_new / correct_two) + 1e-08)
    master_new = master - learn_rate * (update + decay_rate * master)
    ref_new = blend_rate * master_new + (1.0 - blend_rate) * refcopy
    return (master_new, moment_new, second_new, ref_new, master_new.astype(BF16))


def adam_weights(grad, moment, second, master):
    return adam_step(grad, moment, second, master, master)[4]


def place():
    dp, tensor = lax.axis_index("dp"), lax.axis_index("tensor")
    x = dp // 2
    z = (tensor // 8) * 2 + dp % 2
    y = (tensor % 8) // 2
    return x, y, z, tensor % 2


def device(x, y, z, core):
    return (x * 2 + z % 2, (z // 2) * 8 + y * 2 + core)


def group_of(x, z):
    return x * 4 + (z % 2) * 2 + z // 2


def first_row(y):
    return pl.multiple_of(8 * ((5 * y) // 2), 8)


def columns(block, width):
    return pl.ds(pl.multiple_of(block * width, width), width)


def remote(src, dst, send, recv, to):
    return pltpu.make_async_remote_copy(
        src_ref=src, dst_ref=dst, send_sem=send, recv_sem=recv, device_id=to, device_id_type=MESH
    )


def loop(first, last, step):
    def run(i, carry):
        step(i)
        return carry

    lax.fori_loop(first, last, run, 0)


class Near:
    def __init__(self):
        self.x, self.y, self.z, self.core = place()
        x, y, z, core = self.x, self.y, self.z, self.core
        self.dp = x * 2 + z % 2
        self.twin = z % 2
        self.a = x * (1 - core) + z * core
        self.b = x * core + z * (1 - core)
        self.right = device(x, (y + 1) % 4, z, core)
        self.left = device(x, (y + 3) % 4, z, core)
        self.mate = device(x, y, z, 1 - core)
        self.beside = device(x, y, z + 1 - 2 * (z % 2), core)

    def along_a(self, k):
        core = self.core
        return device((self.x + k * (1 - core)) % 4, self.y, (self.z + k * core) % 4, core)

    def along_b(self, k):
        core = self.core
        return device((self.x + k * core) % 4, self.y, (self.z + k * (1 - core)) % 4, core)

    def along_x(self, k):
        return device((self.x + k) % 4, self.y, self.z, self.core)

    def line(self, i):
        py, pc = (self.y + i // 2) % 4, (self.core + i % 2) % 2
        return device(self.x, py, self.z, pc), py, pc

    def group(self, a, b):
        core = self.core
        return group_of(a * (1 - core) + b * core, a * core + b * (1 - core))

    def greet(self):
        barrier = pltpu.get_barrier_semaphore()

        def signal(to):
            pl.semaphore_signal(barrier, inc=1, device_id=to, device_id_type=MESH)

        loop(1, 4, lambda k: signal(self.along_a(k)))
        loop(1, 4, lambda k: signal(self.along_b(k)))
        loop(1, 8, lambda i: signal(self.line(i)[0]))
        pl.semaphore_wait(barrier, 13)


def step_kernel(
    text_hbm, vision_hbm, text_states, vision_states, text_sum, vision_sum, text_out, vision_out,
    mine, other, paired, over_a, over_b, from_left, from_right, total, rest, first_in, first_sum, second_in, reduced,
    rest_part, rest_line, sums, rest_sums, windows, upper, lower_own, lower_in, lower_sum, cross_out, cross_in, lower_x,
    text_state, vision_raw, vision_state, dense, staged, staged_rest, line_in, line_rest, packed,
    text_w, plane, main, rest_w, from_pair,
    load_sem, text_load, state_load, pair_s, pair_r, y_s, y_r, first_s, first_r, second_s, second_r, rest_y_s, rest_y_r,
    win_s, win_r, text_s, text_r, text2_s, text2_r,
    line_s, line_r, plane1_s, plane1_r, plane2_s, plane2_r, back_s, back_r, mate_s, mate_r, spread_s, spread_r,
    own_sem, out_sem,
):
    near = Near()
    x, y, core = near.x, near.y, near.core
    half_rows = text_hbm.shape[0] // 2
    blocks = [(y + 2) % 4, (y + 1) % 4, (y + 3) % 4, y, 4]
    order = (OPP, RIGHT, LEFT, REST, OWN)

    def loads(role):
        cols = columns(blocks[role], COLS)
        return (
            pltpu.make_async_copy(vision_hbm.at[1 - core, :, :, cols], other.at[role], load_sem.at[role, 0]),
            pltpu.make_async_copy(vision_hbm.at[core, :, :, cols], mine.at[role], load_sem.at[role, 1]),
        )

    def text_block(half, block):
        return text_hbm.at[pl.ds(half * half_rows, half_rows), columns(block, COLS)]

    def upper_load(q):
        return pltpu.make_async_copy(text_block(0, 2 * x + q), upper.at[0, q], text_load.at[q])

    def lower_load(px):
        return pltpu.make_async_copy(text_block(1, 2 * px + near.twin), lower_own.at[px], text_load.at[2 + px])

    def state_copies(i):
        return (
            pltpu.make_async_copy(text_states[i], text_state.at[i], state_load.at[i, 0]),
            pltpu.make_async_copy(vision_states[i], vision_raw.at[i], state_load.at[i, 1]),
        )

    for role in order:
        for copy in loads(role):
            copy.start()
    loop(0, 2, lambda q: upper_load(q).start())
    loop(0, 4, lambda px: lower_load(px).start())
    for i in range(3):
        for copy in state_copies(i):
            copy.start()

    near.greet()

    def upper_copy(k, q):
        to = (x + k) % 4
        return remote(
            text_block(0, 2 * to + q), upper.at[k, q], text_s.at[k, q], text_r.at[k, q], near.along_x(k)
        )

    def lower_copy(px):
        return remote(
            text_block(1, 2 * px + 1 - near.twin), lower_in.at[px], text_s.at[4 + px, 0], text_r.at[4 + px, 0],
            near.beside,
        )

    def pair(role):
        return remote(other.at[role], paired.at[role], pair_s.at[role], pair_r.at[role], near.mate)

    for role in order:
        loads(role)[0].wait()
        pair(role).start()

    for k in range(1, 4):
        for q in range(2):
            upper_copy(k, q).start()
    loop(0, 4, lambda px: lower_copy(px).start())

    def ready(role):
        loads(role)[1].wait()
        pair(role).wait_recv()

    def add_pair(role):
        ready(role)

        def add(g):
            both = mine[role, g] + paired[role, g]
            reduced[role, 0, g] = both[:, :TILE]
            reduced[role, 1, g] = both[:, TILE:]

        loop(0, GROUPS, add)

    def add_rest():
        ready(REST)

        def add(i):
            a, b = i // 4, i % 4
            g = near.group(a, b)
            both = mine[REST, g] + paired[REST, g]
            rest[0, a, b] = both[:, :TILE]
            rest[1, a, b] = both[:, TILE:]

        loop(0, GROUPS, add)

    half_a, half_b = pl.ds(0, 8), pl.ds(8, 8)

    def along(tile):
        def go(src, dst, i, to):
            return remote(src, dst, y_s.at[tile, i], y_r.at[tile, i], to)

        return [
            go(reduced.at[OPP, tile, half_a], over_a.at[tile], 0, near.right),
            go(reduced.at[OPP, tile, half_b], over_b.at[tile], 1, near.left),
            go(reduced.at[RIGHT, tile, half_b], from_left.at[tile, half_b], 2, near.right),
            go(reduced.at[LEFT, tile, half_a], from_right.at[tile, half_a], 3, near.left),
            go(reduced.at[RIGHT, tile, half_a], from_left.at[tile, half_a], 4, near.right),
            go(reduced.at[LEFT, tile, half_b], from_right.at[tile, half_b], 5, near.left),
        ]

    line = [along(0), along(1)]

    def pass_on(tile):
        line[tile][0].wait_recv()

        def add_a(g):
            reduced[RIGHT, tile, g] = reduced[RIGHT, tile, g] + over_a[tile, g]

        loop(0, 8, add_a)
        line[tile][4].start()
        line[tile][1].wait_recv()

        def add_b(g):
            reduced[LEFT, tile, 8 + g] = reduced[LEFT, tile, 8 + g] + over_b[tile, g]

        loop(0, 8, add_b)
        line[tile][5].start()

    def add_line(tile):
        for copy in line[tile][2:]:
            copy.wait_recv()

        def add(i):
            a, b = i // 4, i % 4
            g = near.group(a, b)
            total[tile, a, b] = (
                reduced[OWN, tile, g].astype(F32) + from_left[tile, g].astype(F32) + from_right[tile, g].astype(F32)
            ).astype(BF16)

        loop(0, GROUPS, add)

    def source(part):
        return rest.at[part] if part < MAIN_0 else total.at[part - MAIN_0]

    def first_copy(part, k):
        return remote(
            source(part).at[(near.a + k) % 4], first_in.at[part, k], first_s.at[part, k], first_r.at[part, k],
            near.along_a(k),
        )

    def second_copy(part, k):
        return remote(
            first_sum.at[part, (near.b + k) % 4], second_in.at[part, k], second_s.at[part, k], second_r.at[part, k],
            near.along_b(k),
        )

    def first_step(part):
        loop(1, 4, lambda k: first_copy(part, k).start())

    def second_step(part):
        loop(1, 4, lambda k: first_copy(part, k).wait_recv())
        own = source(part).at[near.a]

        def add(b):
            acc = own[b].astype(F32)
            for k in range(1, 4):
                acc = acc + first_in[part, k, b].astype(F32)
            first_sum[part, b] = acc.astype(BF16)

        loop(0, 4, add)
        loop(1, 4, lambda k: second_copy(part, k).start())

    def last_step(part):
        loop(1, 4, lambda k: second_copy(part, k).wait_recv())
        acc = first_sum[part, near.b].astype(F32)
        for k in range(1, 4):
            acc = acc + second_in[part, k].astype(F32)
        return acc

    def cross_copy():
        return remote(cross_out, cross_in, text2_s.at[0], text2_r.at[0], near.beside)

    def lower_x_copy(k):
        return remote(
            lower_sum.at[(x + k) % 4], lower_x.at[k], text2_s.at[k], text2_r.at[k], near.along_x(k)
        )

    def text_middle():
        loop(0, 2, lambda q: upper_load(q).wait())
        for k in range(1, 4):
            for q in range(2):
                upper_copy(k, q).wait_recv()

        def add_upper(i):
            rows = pl.ds(pl.multiple_of(i * 32, 32), 32)
            acc_out = upper[0, 1 - near.twin, rows].astype(F32)
            acc_own = upper[0, near.twin, rows].astype(F32)
            for k in range(1, 4):
                acc_out = acc_out + upper[k, 1 - near.twin, rows].astype(F32)
                acc_own = acc_own + upper[k, near.twin, rows].astype(F32)
            cross_out[rows] = acc_out.astype(BF16)
            text_sum[rows] = acc_own

        loop(0, half_rows // 32, add_upper)
        cross_copy().start()
        loop(0, 4, lambda px: lower_load(px).wait())
        loop(0, 4, lambda px: lower_copy(px).wait_recv())

        def add_lower(i):
            px, rows = i // 4, pl.ds(pl.multiple_of((i % 4) * 64, 64), 64)
            lower_sum[px, rows] = lower_own[px, rows] + lower_in[px, rows]

        loop(0, half_rows // 16, add_lower)
        loop(1, 4, lambda k: lower_x_copy(k).start())

    def text_weights(rows, grad):
        text_sum[rows] = grad
        text_w[rows] = adam_weights(grad, *[text_state[i, rows] for i in range(3)])

    def text_last():
        for i in range(3):
            state_copies(i)[0].wait()
        cross_copy().wait_recv()
        loop(1, 4, lambda k: lower_x_copy(k).wait_recv())

        def add(i):
            rows = pl.ds(pl.multiple_of(i * 32, 32), 32)
            text_weights(rows, text_sum[rows] + cross_in[rows].astype(F32))
            acc = lower_own[x, rows].astype(F32) + lower_in[x, rows].astype(F32)
            for k in range(1, 4):
                acc = acc + lower_x[k, rows].astype(F32)
            text_weights(pl.ds(pl.multiple_of(half_rows + i * 32, 32), 32), acc)

        loop(0, half_rows // 32, add)

    def rest_line_copy(k):
        return remote(
            rest_part, rest_line.at[k], rest_y_s.at[k], rest_y_r.at[k], device(x, (y + k) % 4, near.z, core)
        )

    own_rows = pl.ds(first_row(y), 24)

    def rest_win():
        return remote(
            rest_sums.at[:, own_rows], windows.at[core, pl.ds(8, 2)], win_s.at[0, 0], win_r.at[0, 0], near.mate
        )

    def win_copy(tile, i):
        to, py, _ = near.line(i)
        return remote(
            sums.at[tile, pl.ds(first_row(py), 24)], windows.at[core, 2 * y + tile], win_s.at[tile, i], win_r.at[tile, i],
            to,
        )

    def main_last(tile):
        sums[tile] = last_step(MAIN_0 + tile)
        loop(1, 8, lambda i: win_copy(tile, i).start())
        windows[core, 2 * y + tile] = sums[tile, own_rows]

    def rest_last():
        loop(1, 4, lambda k: rest_line_copy(k).wait_recv())
        for tile in range(2):
            acc = rest_part[tile].astype(F32)
            for k in range(1, 4):
                acc = acc + rest_line[k, tile].astype(F32)
            rest_sums[tile] = acc
            windows[core, 8 + tile] = rest_sums[tile, own_rows]
        rest_win().start()

    def arrange_states():
        for i in range(3):
            state_copies(i)[1].wait()
        for i in range(3):
            for layer in range(2):
                vision_state[i, layer] = jnp.zeros(vision_state.shape[2:], F32)
                for r in range(10):
                    vision_state[i, layer, r : r + 1, :] = vision_raw[i, r, layer : layer + 1, :]
        for layer in range(2):
            dense[layer] = jnp.zeros(dense.shape[1:], F32)

    odd = y % 2 == 1

    def weights_of(tiles):
        for layer in range(2):
            for t in tiles:
                window = windows[layer, t]
                first = jnp.where(odd, window[4:14], window[0:10])
                second = jnp.where(odd, window[14:24], window[10:20])
                dense[layer, 0:10, t * TILE : (t + 1) * TILE] = jnp.where(core == 1, second, first)

        def weights(layer, t):
            cols = slice(t * TILE, (t + 1) * TILE)
            return adam_weights(dense[layer, :, cols], *[vision_state[i, layer, :, cols] for i in range(3)])

        return weights

    def line_copy(tile, i):
        to, py, pc = near.line(i)
        return remote(
            staged.at[tile, pc, py], line_in.at[tile, y * 2 + core], line_s.at[tile, i], line_r.at[tile, i], to
        )

    def line_rest_copy(i):
        to, _, pc = near.line(i)
        return remote(staged_rest.at[pc], line_rest.at[y * 2 + core], line_s.at[2, i], line_r.at[2, i], to)

    def owner_main(tile):
        loop(1, 8, lambda i: win_copy(tile, i).wait_recv())
        weights = weights_of([2 * py + tile for py in range(4)])
        for layer in range(2):
            for py in range(4):
                staged[tile, layer, py] = weights(layer, 2 * py + tile)
        loop(1, 8, lambda i: line_copy(tile, i).start())
        line_in[tile, y * 2 + core] = staged[tile, core, y]

    def owner_rest():
        rest_win().wait_recv()
        weights = weights_of([8, 9])
        for layer in range(2):
            for tile in range(2):
                staged_rest[layer, tile] = weights(layer, 8 + tile)
        loop(1, 8, lambda i: line_rest_copy(i).start())
        line_rest[y * 2 + core] = staged_rest[core]

    def plane1(part, k):
        one = plane.at[part, near.a, near.b]
        return remote(one, one, plane1_s.at[part, k], plane1_r.at[part, k], near.along_b(k))

    def plane2(part, k):
        row = plane.at[part, near.a]
        return remote(row, row, plane2_s.at[part, k], plane2_r.at[part, k], near.along_a(k))

    def pack(part, rows_of):
        for i in range(8):
            packed[part, 10 * i : 10 * i + 10, :] = rows_of(i).astype(F32)[:10]
        plane[part, near.a, near.b] = packed[part].astype(BF16)
        loop(1, 4, lambda k: plane1(part, k).start())

    def pack_main(tile):
        loop(1, 8, lambda i: line_copy(tile, i).wait_recv())
        pack(MAIN_0 + tile, lambda i: line_in[tile, i])

    def pack_rest():
        loop(1, 8, lambda i: line_rest_copy(i).wait_recv())
        for tile in range(2):
            pack(REST_0 + tile, lambda i: line_rest[i, tile])

    def across(part):
        loop(1, 4, lambda k: plane1(part, k).wait_recv())
        loop(1, 4, lambda k: plane2(part, k).start())

    def spread(part, dst):
        loop(1, 4, lambda k: plane2(part, k).wait_recv())

        def move(i):
            a, b = i // 4, i % 4
            dst[near.group(a, b)] = plane[part, a, b]

        loop(0, GROUPS, move)

    def back(tile):
        def go(src, dst, half, i, to):
            return remote(main.at[src, tile, half], main.at[dst, tile, half], back_s.at[tile, i], back_r.at[tile, i], to)

        return [
            go(OWN, LEFT, half_a, 0, near.right),
            go(OWN, RIGHT, half_b, 1, near.left),
            go(OWN, LEFT, half_b, 2, near.right),
            go(OWN, RIGHT, half_a, 3, near.left),
            go(LEFT, OPP, half_a, 4, near.right),
            go(RIGHT, OPP, half_b, 5, near.left),
        ]

    ways = [back(0), back(1)]
    tiles = {OPP: 2 * blocks[OPP], RIGHT: 2 * blocks[RIGHT], LEFT: 2 * blocks[LEFT], OWN: 2 * y, REST: 8}

    def held(role, tile):
        return rest_w.at[tile] if role == REST else main.at[role, tile]

    def mate(role, tile):
        return remote(
            held(role, tile), from_pair.at[role, tile], mate_s.at[role, tile], mate_r.at[role, tile], near.mate
        )

    def write(role, tile, which):
        src = from_pair.at[role, tile] if which else held(role, tile)
        layer = 1 - core if which else core
        cols = columns(tiles[role] + tile, TILE)
        return pltpu.make_async_copy(src, vision_out.at[layer, :, :, cols], out_sem.at[role, tile, which])

    def give(role, tile):
        mate(role, tile).start()
        write(role, tile, 0).start()

    upper_rows, lower_rows = pl.ds(0, half_rows), pl.ds(half_rows, half_rows)
    own_cols = columns(near.dp, COLS)

    def own_text():
        return pltpu.make_async_copy(text_w, text_out.at[:, own_cols], own_sem)

    def beside_copy():
        return remote(
            text_w.at[upper_rows], text_out.at[upper_rows, own_cols], spread_s.at[0, 0], spread_r.at[0, 0], near.beside
        )

    def x_copy(k):
        return remote(
            text_w.at[lower_rows], text_out.at[lower_rows, own_cols], spread_s.at[0, k], spread_r.at[0, k],
            near.along_x(k),
        )

    def upper_on(k):
        both = text_out.at[upper_rows, columns(x, 2 * COLS)]
        return remote(both, both, spread_s.at[1, k], spread_r.at[1, k], near.along_x(k))

    def lower_on(px):
        one = text_out.at[lower_rows, columns(2 * px + near.twin, COLS)]
        return remote(one, one, spread_s.at[2, px], spread_r.at[2, px], near.beside)

    def text_spread():
        own_text().start()
        beside_copy().start()
        loop(1, 4, lambda k: x_copy(k).start())

    def text_spread_on():
        own_text().wait()
        beside_copy().wait_recv()
        loop(1, 4, lambda k: upper_on(k).start())
        loop(1, 4, lambda k: x_copy(k).wait_recv())
        loop(0, 4, lambda px: lower_on(px).start())

    add_pair(OPP)
    line[0][0].start()
    line[0][1].start()
    add_pair(RIGHT)
    line[0][2].start()
    add_pair(LEFT)
    line[0][3].start()
    add_rest()
    first_step(REST_0)
    first_step(REST_1)
    add_pair(OWN)
    pass_on(0)
    for copy in line[1][:4]:
        copy.start()
    arrange_states()
    second_step(REST_0)
    second_step(REST_1)
    add_line(0)
    first_step(MAIN_0)
    pass_on(1)
    text_middle()
    for tile in range(2):
        rest_part[tile] = last_step(REST_0 + tile).astype(BF16)
    loop(1, 4, lambda k: rest_line_copy(k).start())
    second_step(MAIN_0)
    rest_last()
    main_last(0)
    text_last()
    text_spread()
    owner_main(0)
    add_line(1)
    first_step(MAIN_1)
    owner_rest()
    pack_main(0)
    second_step(MAIN_1)
    across(MAIN_0)
    pack_rest()
    main_last(1)
    text_spread_on()
    spread(MAIN_0, main.at[OWN, 0])
    for copy in ways[0][:4]:
        copy.start()
    owner_main(1)
    across(REST_0)
    across(REST_1)
    give(OWN, 0)
    pack_main(1)
    ways[0][0].wait_recv()
    ways[0][4].start()
    ways[0][1].wait_recv()
    ways[0][5].start()
    across(MAIN_1)
    for tile in range(2):
        spread(REST_0 + tile, rest_w.at[tile])
        give(REST, tile)
    spread(MAIN_1, main.at[OWN, 1])
    for copy in ways[1][:4]:
        copy.start()
    give(OWN, 1)

    for tile in range(2):
        ways[tile][2].wait_recv()
        give(LEFT, tile)
        ways[tile][3].wait_recv()
        give(RIGHT, tile)
        if tile == 0:
            ways[1][0].wait_recv()
            ways[1][4].start()
            ways[1][1].wait_recv()
            ways[1][5].start()
        ways[tile][4].wait_recv()
        ways[tile][5].wait_recv()
        give(OPP, tile)

    for r in range(10):
        for layer in range(2):
            vision_sum[r, layer : layer + 1, :] = dense[layer, r : r + 1, :]
    for role in order:
        pair(role).wait_send()
    for copy in line[0] + line[1]:
        copy.wait_send()
    for k in range(1, 4):
        for q in range(2):
            upper_copy(k, q).wait_send()
    loop(0, 4, lambda px: lower_copy(px).wait_send())
    cross_copy().wait_send()
    loop(1, 4, lambda k: lower_x_copy(k).wait_send())
    for part in range(4):
        loop(1, 4, lambda k: first_copy(part, k).wait_send())
        loop(1, 4, lambda k: second_copy(part, k).wait_send())
        loop(1, 4, lambda k: plane1(part, k).wait_send())
        loop(1, 4, lambda k: plane2(part, k).wait_send())
    loop(1, 4, lambda k: rest_line_copy(k).wait_send())
    rest_win().wait_send()
    for tile in range(2):
        loop(1, 8, lambda i: win_copy(tile, i).wait_send())
        loop(1, 8, lambda i: line_copy(tile, i).wait_send())
    loop(1, 8, lambda i: line_rest_copy(i).wait_send())
    beside_copy().wait_send()
    loop(1, 4, lambda k: x_copy(k).wait_send())
    loop(1, 4, lambda k: upper_on(k).wait())
    loop(0, 4, lambda px: lower_on(px).wait())
    arrivals = [(OWN, 0), (REST, 0), (REST, 1), (OWN, 1), (LEFT, 0), (RIGHT, 0), (OPP, 0), (LEFT, 1), (RIGHT, 1), (OPP, 1)]
    for role, tile in arrivals:
        mate(role, tile).wait_recv()
        write(role, tile, 1).start()
    for copy in ways[0] + ways[1]:
        copy.wait_send()
    for role, tile in arrivals:
        mate(role, tile).wait_send()
        write(role, tile, 0).wait()
        write(role, tile, 1).wait()


def kernel_of(given):
    def run(text_hbm, vision_hbm, *refs):
        given(text_hbm, vision_hbm, refs[:3], refs[3:6], *refs[6:])

    return run


def step(text, vision, text_states, vision_states):
    rows = text.shape[0]
    half = rows // 2
    block = (GROUPS, ROWS, COLS)
    tile = (GROUPS, ROWS, TILE)
    square = (4, 4, ROWS, TILE)
    dma = pltpu.SemaphoreType.DMA
    vmem = pltpu.VMEM
    return pl.pallas_call(
        kernel_of(step_kernel),
        name="sum_step_gather",
        out_shape=(
            jax.ShapeDtypeStruct((rows, COLS), F32),
            jax.ShapeDtypeStruct(vision_states[0].shape, F32),
            jax.ShapeDtypeStruct((rows, 8 * COLS), BF16),
            jax.ShapeDtypeStruct((2, GROUPS, ROWS, 5 * COLS), BF16),
        ),
        in_specs=[pl.BlockSpec(memory_space=pltpu.HBM)] * 8,
        out_specs=[pl.BlockSpec(memory_space=pltpu.VMEM)] * 2 + [pl.BlockSpec(memory_space=pltpu.HBM)] * 2,
        scratch_shapes=[
            vmem((5,) + block, BF16),
            vmem((5,) + block, BF16),
            vmem((5,) + block, BF16),
            vmem((2, 8, ROWS, TILE), BF16),
            vmem((2, 8, ROWS, TILE), BF16),
            vmem((2,) + tile, BF16),
            vmem((2,) + tile, BF16),
            vmem((2,) + square, BF16),
            vmem((2,) + square, BF16),
            vmem((4,) + square, BF16),
            vmem((4, 4, ROWS, TILE), BF16),
            vmem((4, 4, ROWS, TILE), BF16),
            vmem((4, 2) + tile, BF16),
            vmem((2, ROWS, TILE), BF16),
            vmem((4, 2, ROWS, TILE), BF16),
            vmem((2, ROWS, TILE), F32),
            vmem((2, ROWS, TILE), F32),
            vmem((2, 10, 24, TILE), F32),
            vmem((4, 2, half, COLS), BF16),
            vmem((4, half, COLS), BF16),
            vmem((4, half, COLS), BF16),
            vmem((4, half, COLS), BF16),
            vmem((half, COLS), BF16),
            vmem((half, COLS), BF16),
            vmem((4, half, COLS), BF16),
            vmem((3, rows, COLS), F32),
            vmem((3,) + vision_states[0].shape, F32),
            vmem((3, 2, 16, 5 * COLS), F32),
            vmem((2, 16, 5 * COLS), F32),
            vmem((2, 2, 4, 16, TILE), BF16),
            vmem((2, 2, 16, TILE), BF16),
            vmem((2, 8, 16, TILE), BF16),
            vmem((8, 2, 16, TILE), BF16),
            vmem((4, ROWS, TILE), F32),
            vmem((rows, COLS), BF16),
            vmem((4,) + square, BF16),
            vmem((4, 2) + tile, BF16),
            vmem((2,) + tile, BF16),
            vmem((5, 2) + tile, BF16),
            dma((5, 2)),
            dma((6,)),
            dma((3, 2)),
            dma((5,)), dma((5,)),
            dma((2, 6)), dma((2, 6)),
            dma((4, 4)), dma((4, 4)),
            dma((4, 4)), dma((4, 4)),
            dma((4,)), dma((4,)),
            dma((2, 8)), dma((2, 8)),
            dma((8, 2)), dma((8, 2)),
            dma((4,)), dma((4,)),
            dma((3, 8)), dma((3, 8)),
            dma((4, 4)), dma((4, 4)),
            dma((4, 4)), dma((4, 4)),
            dma((2, 6)), dma((2, 6)),
            dma((5, 2)), dma((5, 2)),
            dma((3, 4)), dma((3, 4)),
            dma,
            dma((5, 2, 2)),
        ],
        compiler_params=pltpu.CompilerParams(collective_id=1, has_side_effects=True, vmem_limit_bytes=40 << 20),
    )(*[pltpu.with_memory_space_constraint(array, pltpu.HBM) for array in (text, vision, *text_states, *vision_states)])


def finish_kernel(*refs):
    text, vision, text_full, vision_full = refs[:5], refs[5:10], refs[10], refs[11]
    outs, vision_w = refs[12:22], refs[21]
    text_made, vision_made, sem = refs[22:]
    text_w = outs[4]
    copies = [
        pltpu.make_async_copy(vision_full, vision_w, sem.at[0]),
        pltpu.make_async_copy(text_full, text_w, sem.at[1]),
    ]
    for copy in copies:
        copy.start()

    def one(i):
        rows = pl.ds(pl.multiple_of(i * 32, 32), 32)
        made = adam_step(*[ref[rows] for ref in text])
        for j in range(4):
            text_made[j, rows] = made[j]

    loop(0, text_made.shape[1] // 32, one)
    for j in range(4):
        copies.append(pltpu.make_async_copy(text_made.at[j], outs[j], sem.at[2 + j]))
        copies[-1].start()

    def row(r):
        made = adam_step(*[ref[r] for ref in vision])
        for j in range(4):
            vision_made[j, r] = made[j]

    loop(0, vision_made.shape[1], row)
    for j in range(4):
        copies.append(pltpu.make_async_copy(vision_made.at[j], outs[5 + j], sem.at[6 + j]))
        copies[-1].start()
    for copy in copies:
        copy.wait()


def finish(text, vision, text_full, vision_full):
    def like(array):
        return jax.ShapeDtypeStruct(array.shape, array.dtype)

    in_hbm, in_vmem = pl.BlockSpec(memory_space=pltpu.HBM), pl.BlockSpec(memory_space=pltpu.VMEM)
    return pl.pallas_call(
        finish_kernel,
        name="write_results",
        out_shape=(like(text[0]),) * 4 + (like(text_full),) + (like(vision[0]),) * 4 + (like(vision_full),),
        in_specs=[in_vmem] * 10 + [in_hbm] * 2,
        out_specs=[in_hbm] * 10,
        scratch_shapes=[
            pltpu.VMEM((4,) + text[0].shape, F32),
            pltpu.VMEM((4,) + vision[0].shape, F32),
            pltpu.SemaphoreType.DMA((10,)),
        ],
        compiler_params=pltpu.CompilerParams(vmem_limit_bytes=16 << 20),
    )(*text, *vision, text_full, vision_full)


def body(
    text_grads, text_master, text_moment, text_second, text_ref,
    vision_grads, vision_master, vision_moment, vision_second, vision_ref,
):
    layers, width = vision_grads.shape[1], vision_grads.shape[3]
    text_states = (text_moment, text_second, text_master, text_ref)
    vision_states = tuple(
        jnp.transpose(array, (1, 0, 2)) for array in (vision_moment, vision_second, vision_master, vision_ref)
    )
    text_total, vision_total, text_full, vision_full = step(
        text_grads[0], vision_grads.reshape(layers, GROUPS, ROWS, width), text_states[:3], vision_states[:3]
    )
    outs = finish((text_total,) + text_states, (vision_total,) + vision_states, text_full, vision_full)
    vision_out = tuple(jnp.transpose(array, (1, 0, 2)) for array in outs[5:9])
    return outs[:5] + vision_out + (outs[9].reshape(layers, width, width),)


def solution(mesh):
    owned = P("tensor", "dp")
    vision_owned = P(None, ("dp", "tensor"), None)
    return jax.shard_map(
        body,
        mesh=mesh,
        in_specs=(P("dp", "tensor", None),) + (owned,) * 4 + (P(("dp", "tensor"), None, None, None),) + (vision_owned,) * 4,
        out_specs=(owned,) * 4 + (P("tensor", None),) + (vision_owned,) * 4 + (P(),),
        check_vma=False,
    )
```

time: 105 us -> 96.6 us (0.920)
  local copies, waits for them, and re-layouts: 7.04 us -> 0.03 us
  other arithmetic: 4.41 us -> 0 us
  Pallas kernels: 92.3 us -> 95.7 us
    unnamed x24 -> x16, local copies, waits for them, and re-layouts: 7.03 us -> 0.03 us
    pallas_call x2, Pallas kernels: 92.3 us -> 95.7 us  [the longest x1 91.5 us: step(): pl.pallas_call(kernel_of(step_kernel), name='sum_step_gather', out_shape=...]
    convert_element_type x2 -> x0, other arithmetic: 2.43 us -> none  [adam_step(): master_new.astype(BF16)]
    add x2 -> x0, other arithmetic: 1.98 us -> none  [adam_step(): ref_new = blend_rate * master_new + (1.0 - blend_rate) * refcopy]
where the time goes in v3:
time: 96.6 us; the launch traced here: 96.5 us
  Pallas kernels  95.7 us (99%)
    pallas_call x1, Pallas kernels, step(): pl.pallas_call(kernel_of(step_kernel), name='sum_step_gather', out_shape=...  91.5 us
    pallas_call x1, Pallas kernels, finish(): pl.pallas_call(finish_kernel, name='write_results', out_shape=(like(text[...  4.25 us

profile of v3, /device:TPU:1, one launch (start us, length us, event | category | flops | bytes accessed | tf_op | source)
XLA Modules:
  0.0 96.5 jit_solution(14578644656951759461)
XLA Ops:
  0.6 0.0 copy-start.1
  0.7 0.0 copy-start
  0.7 0.0 copy-start.2
  0.7 0.0 copy-start.7
  0.7 0.0 copy-start.5
  0.7 0.0 copy-start.4
  0.7 0.0 copy-start.6
  0.7 0.0 copy-start.3
  0.7 91.5 %sum_step_gather.1 = (f32[512,256]{1,0:T(8,128)S(1)}, f32[10,2,1280]{2,1,0:T(2,128)S(1)}, bf16[512,2048]{1,0:T(8,128)(2,1)S(1)}, bf16[2,16,80,1280]{3,2,1,0:T(8,128)(2,1)S(1)}) custom-call(bf16[512,2048]{1,0:T(8,128)(2,1)} %bitcast.19, bf16[2,16,80,1280]{3,2,1,0:T(8,128)(2,1)} %bitcast.18, f32[512,256]{1,0:T(8,128)} %refs_1_.3, f32[512,256]{1,0:T(8,128)} %refs_2_.3, ...), custom_call_target="tpu_custom_call" | custom-call | tf_op jit(solution)/shard_map/sum_step_gather/pallas_call | solution.py:689
  92.2 0.0 copy-done.1
  92.2 0.0 copy-done
  92.2 0.0 copy-done.2
  92.2 0.0 copy-done.7
  92.2 0.0 copy-done.5
  92.2 0.0 copy-done.4
  92.3 0.0 copy-done.6
  92.3 0.0 copy-done.3
  92.3 4.2 %write_results.1 = (f32[512,256]{1,0:T(8,128)}, f32[512,256]{1,0:T(8,128)}, f32[512,256]{1,0:T(8,128)}, f32[512,256]{1,0:T(8,128)}, bf16[512,2048]{1,0:T(8,128)(...) custom-call(f32[512,256]{1,0:T(8,128)S(1)} %get-tuple-element.24.ref, ...), custom_call_target="tpu_custom_call" | custom-call | tf_op jit(solution)/shard_map/write_results/pallas_call | solution.py:805
Async XLA Ops:
  0.6 91.5 %copy-start.1 = (f32[512,256]{1,0:T(8,128)S(1)}, f32[512,256]{1,0:T(8,128)}, u32[]{:S(2)}) copy-start(f32[512,256]{1,0:T(8,128)} %refs_2_.3) | copy-start | bytes 1572868
  0.7 91.5 %copy-start = (f32[512,256]{1,0:T(8,128)S(1)}, f32[512,256]{1,0:T(8,128)}, u32[]{:S(2)}) copy-start(f32[512,256]{1,0:T(8,128)} %refs_1_.3) | copy-start | bytes 1572868
  0.7 91.5 %copy-start.2 = (f32[512,256]{1,0:T(8,128)S(1)}, f32[512,256]{1,0:T(8,128)}, u32[]{:S(2)}) copy-start(f32[512,256]{1,0:T(8,128)} %refs_3_.1) | copy-start | bytes 1572868
  0.7 91.5 %copy-start.7 = (f32[2,10,1280]{2,0,1:T(2,128)S(1)}, f32[2,10,1280]{2,0,1:T(2,128)}, u32[]{:S(2)}) copy-start(f32[2,10,1280]{2,0,1:T(2,128)} %param.19) | copy-start | bytes 307204
  0.7 91.5 %copy-start.5 = (f32[2,10,1280]{2,0,1:T(2,128)S(1)}, f32[2,10,1280]{2,0,1:T(2,128)}, u32[]{:S(2)}) copy-start(f32[2,10,1280]{2,0,1:T(2,128)} %param.18) | copy-start | bytes 307204
  0.7 91.5 %copy-start.4 = (f32[2,10,1280]{2,0,1:T(2,128)S(1)}, f32[2,10,1280]{2,0,1:T(2,128)}, u32[]{:S(2)}) copy-start(f32[2,10,1280]{2,0,1:T(2,128)} %param.17) | copy-start | bytes 307204
  0.7 91.5 %copy-start.6 = (f32[2,10,1280]{2,0,1:T(2,128)S(1)}, f32[2,10,1280]{2,0,1:T(2,128)}, u32[]{:S(2)}) copy-start(f32[2,10,1280]{2,0,1:T(2,128)} %param.16) | copy-start | bytes 307204
  0.7 91.5 %copy-start.3 = (f32[512,256]{1,0:T(8,128)S(1)}, f32[512,256]{1,0:T(8,128)}, u32[]{:S(2)}) copy-start(f32[512,256]{1,0:T(8,128)} %refs_4_.1) | copy-start | bytes 1572868

commit v4 on v3

--- a/solution.py
+++ b/solution.py
@@ -124,13 +124,12 @@
 def step_kernel(
     text_hbm, vision_hbm, text_states, vision_states, text_sum, vision_sum, text_out, vision_out,
     mine, other, paired, over_a, over_b, from_left, from_right, total, rest, first_in, first_sum, second_in, reduced,
-    rest_part, rest_line, sums, rest_sums, windows, upper, lower_own, lower_in, lower_sum, cross_out, cross_in, lower_x,
-    text_state, vision_raw, vision_state, dense, staged, staged_rest, line_in, line_rest, packed,
-    text_w, plane, main, rest_w, from_pair,
-    load_sem, text_load, state_load, pair_s, pair_r, y_s, y_r, first_s, first_r, second_s, second_r, rest_y_s, rest_y_r,
-    win_s, win_r, text_s, text_r, text2_s, text2_r,
+    sums, rest_sums, windows, rest_windows, upper, lower_own, lower_in, lower_sum, cross_out, cross_in, lower_x,
+    text_state, vision_raw, own_state, line_state, tile_state, dense, staged_rest, line_rest, packed, text_w, plane,
+    load_sem, text_load, state_load, pair_s, pair_r, y_s, y_r, first_s, first_r, second_s, second_r,
+    state_s, state_r, win_s, win_r, rest_win_s, rest_win_r, text_s, text_r, text2_s, text2_r,
     line_s, line_r, plane1_s, plane1_r, plane2_s, plane2_r, back_s, back_r, mate_s, mate_r, spread_s, spread_r,
-    own_sem, out_sem,
+    own_sem,
 ):
     near = Near()
     x, y, core = near.x, near.y, near.core
@@ -160,14 +159,17 @@
             pltpu.make_async_copy(vision_states[i], vision_raw.at[i], state_load.at[i, 1]),
         )
 
-    for role in order:
+    for copy in loads(OPP):
+        copy.start()
+    for i in range(3):
+        state_copies(i)[1].start()
+    for role in order[1:]:
         for copy in loads(role):
             copy.start()
     loop(0, 2, lambda q: upper_load(q).start())
     loop(0, 4, lambda px: lower_load(px).start())
     for i in range(3):
-        for copy in state_copies(i):
-            copy.start()
+        state_copies(i)[0].start()
 
     near.greet()
 
@@ -185,15 +187,6 @@
 
     def pair(role):
         return remote(other.at[role], paired.at[role], pair_s.at[role], pair_r.at[role], near.mate)
-
-    for role in order:
-        loads(role)[0].wait()
-        pair(role).start()
-
-    for k in range(1, 4):
-        for q in range(2):
-            upper_copy(k, q).start()
-    loop(0, 4, lambda px: lower_copy(px).start())
 
     def ready(role):
         loads(role)[1].wait()
@@ -361,94 +354,96 @@
 
         loop(0, half_rows // 32, add)
 
-    def rest_line_copy(k):
-        return remote(
-            rest_part, rest_line.at[k], rest_y_s.at[k], rest_y_r.at[k], device(x, (y + k) % 4, near.z, core)
-        )
-
-    own_rows = pl.ds(first_row(y), 24)
-
-    def rest_win():
-        return remote(
-            rest_sums.at[:, own_rows], windows.at[core, pl.ds(8, 2)], win_s.at[0, 0], win_r.at[0, 0], near.mate
-        )
-
-    def win_copy(tile, i):
-        to, py, _ = near.line(i)
-        return remote(
-            sums.at[tile, pl.ds(first_row(py), 24)], windows.at[core, 2 * y + tile], win_s.at[tile, i], win_r.at[tile, i],
-            to,
-        )
-
-    def main_last(tile):
-        sums[tile] = last_step(MAIN_0 + tile)
-        loop(1, 8, lambda i: win_copy(tile, i).start())
-        windows[core, 2 * y + tile] = sums[tile, own_rows]
-
-    def rest_last():
-        loop(1, 4, lambda k: rest_line_copy(k).wait_recv())
-        for tile in range(2):
-            acc = rest_part[tile].astype(F32)
-            for k in range(1, 4):
-                acc = acc + rest_line[k, tile].astype(F32)
-            rest_sums[tile] = acc
-            windows[core, 8 + tile] = rest_sums[tile, own_rows]
-        rest_win().start()
-
     def arrange_states():
         for i in range(3):
             state_copies(i)[1].wait()
-        for i in range(3):
-            for layer in range(2):
-                vision_state[i, layer] = jnp.zeros(vision_state.shape[2:], F32)
+        for layer in range(2):
+            for i in range(3):
                 for r in range(10):
-                    vision_state[i, layer, r : r + 1, :] = vision_raw[i, r, layer : layer + 1, :]
-        for layer in range(2):
-            dense[layer] = jnp.zeros(dense.shape[1:], F32)
+                    own_state[layer, 10 * i + r : 10 * i + r + 1, :] = vision_raw[i, r, layer : layer + 1, :]
+
+    def state_copy(i):
+        to, py, pc = near.line(i)
+        return remote(
+            own_state.at[pc, :, columns(py, COLS)], line_state.at[y * 2 + core], state_s.at[i], state_r.at[i], to
+        )
+
+    def send_states():
+        loop(1, 8, lambda i: state_copy(i).start())
+        line_state[y * 2 + core] = own_state[core, :, columns(y, COLS)]
+
+    def join_states():
+        loop(1, 8, lambda i: state_copy(i).wait_recv())
+        for place_on_line in range(8):
+            for i in range(3):
+                tile_state[i, 10 * place_on_line : 10 * place_on_line + 10, :] = line_state[
+                    place_on_line, 10 * i : 10 * i + 10, :
+                ]
+
+    own_rows = pl.ds(first_row(y), 24)
+
+    def win_copy(tile, i):
+        to, py, _ = near.line(i)
+        return remote(
+            sums.at[tile, pl.ds(first_row(py), 24)], windows.at[core, 2 * y + tile], win_s.at[tile, i], win_r.at[tile, i],
+            to,
+        )
+
+    def rest_win_copy(i):
+        to, py, _ = near.line(i)
+        return remote(
+            rest_sums.at[:, pl.ds(first_row(py), 24)], rest_windows.at[core, y], rest_win_s.at[i], rest_win_r.at[i], to
+        )
+
+    def main_last(tile):
+        part = MAIN_0 + tile
+        grad = last_step(part)
+        sums[tile] = grad
+        cols = slice(tile * TILE, (tile + 1) * TILE)
+        plane[part, near.a, near.b] = adam_weights(grad, *[tile_state[i, :, cols] for i in range(3)])
+        loop(1, 4, lambda k: plane1(part, k).start())
+        loop(1, 8, lambda i: win_copy(tile, i).start())
+        windows[core, 2 * y + tile] = sums[tile, own_rows]
+
+    def rest_last():
+        for tile in range(2):
+            rest_sums[tile] = last_step(REST_0 + tile)
+        loop(1, 8, lambda i: rest_win_copy(i).start())
+        rest_windows[core, y] = rest_sums[:, own_rows]
 
     odd = y % 2 == 1
 
-    def weights_of(tiles):
-        for layer in range(2):
-            for t in tiles:
-                window = windows[layer, t]
-                first = jnp.where(odd, window[4:14], window[0:10])
-                second = jnp.where(odd, window[14:24], window[10:20])
-                dense[layer, 0:10, t * TILE : (t + 1) * TILE] = jnp.where(core == 1, second, first)
-
-        def weights(layer, t):
-            cols = slice(t * TILE, (t + 1) * TILE)
-            return adam_weights(dense[layer, :, cols], *[vision_state[i, layer, :, cols] for i in range(3)])
-
-        return weights
-
-    def line_copy(tile, i):
-        to, py, pc = near.line(i)
-        return remote(
-            staged.at[tile, pc, py], line_in.at[tile, y * 2 + core], line_s.at[tile, i], line_r.at[tile, i], to
-        )
+    def own_part(window):
+        first = jnp.where(odd, window[4:14], window[0:10])
+        second = jnp.where(odd, window[14:24], window[10:20])
+        return jnp.where(core == 1, second, first)
 
     def line_rest_copy(i):
         to, _, pc = near.line(i)
-        return remote(staged_rest.at[pc], line_rest.at[y * 2 + core], line_s.at[2, i], line_r.at[2, i], to)
+        return remote(staged_rest.at[pc], line_rest.at[y * 2 + core], line_s.at[i], line_r.at[i], to)
+
+    def owner_rest():
+        loop(1, 8, lambda i: rest_win_copy(i).wait_recv())
+        for layer in range(2):
+            for tile in range(2):
+                cols = slice((8 + tile) * TILE, (9 + tile) * TILE)
+                window = rest_windows[layer, 0, tile]
+                for py in range(1, 4):
+                    window = window + rest_windows[layer, py, tile]
+                grad = own_part(window)
+                dense[layer, 0:10, cols] = grad
+                staged_rest[layer, tile, 0:10] = adam_weights(
+                    grad, *[own_state[layer, 10 * i : 10 * i + 10, cols] for i in range(3)]
+                )
+        loop(1, 8, lambda i: line_rest_copy(i).start())
+        line_rest[y * 2 + core] = staged_rest[core]
 
     def owner_main(tile):
         loop(1, 8, lambda i: win_copy(tile, i).wait_recv())
-        weights = weights_of([2 * py + tile for py in range(4)])
         for layer in range(2):
             for py in range(4):
-                staged[tile, layer, py] = weights(layer, 2 * py + tile)
-        loop(1, 8, lambda i: line_copy(tile, i).start())
-        line_in[tile, y * 2 + core] = staged[tile, core, y]
-
-    def owner_rest():
-        rest_win().wait_recv()
-        weights = weights_of([8, 9])
-        for layer in range(2):
-            for tile in range(2):
-                staged_rest[layer, tile] = weights(layer, 8 + tile)
-        loop(1, 8, lambda i: line_rest_copy(i).start())
-        line_rest[y * 2 + core] = staged_rest[core]
+                t = 2 * py + tile
+                dense[layer, 0:10, t * TILE : (t + 1) * TILE] = own_part(windows[layer, t])
 
     def plane1(part, k):
         one = plane.at[part, near.a, near.b]
@@ -458,67 +453,54 @@
         row = plane.at[part, near.a]
         return remote(row, row, plane2_s.at[part, k], plane2_r.at[part, k], near.along_a(k))
 
-    def pack(part, rows_of):
-        for i in range(8):
-            packed[part, 10 * i : 10 * i + 10, :] = rows_of(i).astype(F32)[:10]
-        plane[part, near.a, near.b] = packed[part].astype(BF16)
-        loop(1, 4, lambda k: plane1(part, k).start())
-
-    def pack_main(tile):
-        loop(1, 8, lambda i: line_copy(tile, i).wait_recv())
-        pack(MAIN_0 + tile, lambda i: line_in[tile, i])
-
     def pack_rest():
         loop(1, 8, lambda i: line_rest_copy(i).wait_recv())
         for tile in range(2):
-            pack(REST_0 + tile, lambda i: line_rest[i, tile])
+            part = REST_0 + tile
+            for i in range(8):
+                packed[tile, 10 * i : 10 * i + 10, :] = line_rest[i, tile].astype(F32)[:10]
+            plane[part, near.a, near.b] = packed[tile].astype(BF16)
+            loop(1, 4, lambda k: plane1(part, k).start())
 
     def across(part):
         loop(1, 4, lambda k: plane1(part, k).wait_recv())
         loop(1, 4, lambda k: plane2(part, k).start())
 
-    def spread(part, dst):
+    first_tile = {OPP: 2 * blocks[OPP], RIGHT: 2 * blocks[RIGHT], LEFT: 2 * blocks[LEFT], OWN: 2 * y, REST: 8}
+
+    def held(role, tile):
+        return vision_out.at[core, first_tile[role] + tile]
+
+    def spread(part, role, tile):
         loop(1, 4, lambda k: plane2(part, k).wait_recv())
 
         def move(i):
             a, b = i // 4, i % 4
-            dst[near.group(a, b)] = plane[part, a, b]
+            vision_out[core, first_tile[role] + tile, near.group(a, b)] = plane[part, a, b]
 
         loop(0, GROUPS, move)
 
     def back(tile):
-        def go(src, dst, half, i, to):
-            return remote(main.at[src, tile, half], main.at[dst, tile, half], back_s.at[tile, i], back_r.at[tile, i], to)
+        def go(role, half, i, to):
+            part = held(role, tile).at[half]
+            return remote(part, part, back_s.at[tile, i], back_r.at[tile, i], to)
 
         return [
-            go(OWN, LEFT, half_a, 0, near.right),
-            go(OWN, RIGHT, half_b, 1, near.left),
-            go(OWN, LEFT, half_b, 2, near.right),
-            go(OWN, RIGHT, half_a, 3, near.left),
-            go(LEFT, OPP, half_a, 4, near.right),
-            go(RIGHT, OPP, half_b, 5, near.left),
+            go(OWN, half_a, 0, near.right),
+            go(OWN, half_b, 1, near.left),
+            go(OWN, half_b, 2, near.right),
+            go(OWN, half_a, 3, near.left),
+            go(LEFT, half_a, 4, near.right),
+            go(RIGHT, half_b, 5, near.left),
         ]
 
     ways = [back(0), back(1)]
-    tiles = {OPP: 2 * blocks[OPP], RIGHT: 2 * blocks[RIGHT], LEFT: 2 * blocks[LEFT], OWN: 2 * y, REST: 8}
-
-    def held(role, tile):
-        return rest_w.at[tile] if role == REST else main.at[role, tile]
 
     def mate(role, tile):
-        return remote(
-            held(role, tile), from_pair.at[role, tile], mate_s.at[role, tile], mate_r.at[role, tile], near.mate
-        )
-
-    def write(role, tile, which):
-        src = from_pair.at[role, tile] if which else held(role, tile)
-        layer = 1 - core if which else core
-        cols = columns(tiles[role] + tile, TILE)
-        return pltpu.make_async_copy(src, vision_out.at[layer, :, :, cols], out_sem.at[role, tile, which])
+        return remote(held(role, tile), held(role, tile), mate_s.at[role, tile], mate_r.at[role, tile], near.mate)
 
     def give(role, tile):
         mate(role, tile).start()
-        write(role, tile, 0).start()
 
     upper_rows, lower_rows = pl.ds(0, half_rows), pl.ds(half_rows, half_rows)
     own_cols = columns(near.dp, COLS)
@@ -557,6 +539,16 @@
         loop(1, 4, lambda k: x_copy(k).wait_recv())
         loop(0, 4, lambda px: lower_on(px).start())
 
+    def start_pair(role):
+        loads(role)[0].wait()
+        pair(role).start()
+
+    for k in range(1, 4):
+        for q in range(2):
+            upper_copy(k, q).start()
+    loop(0, 4, lambda px: lower_copy(px).start())
+    for role in order:
+        start_pair(role)
     add_pair(OPP)
     line[0][0].start()
     line[0][1].start()
@@ -572,68 +564,62 @@
     for copy in line[1][:4]:
         copy.start()
     arrange_states()
+    send_states()
+    add_line(0)
+    first_step(MAIN_0)
     second_step(REST_0)
     second_step(REST_1)
-    add_line(0)
-    first_step(MAIN_0)
     pass_on(1)
+    second_step(MAIN_0)
     text_middle()
-    for tile in range(2):
-        rest_part[tile] = last_step(REST_0 + tile).astype(BF16)
-    loop(1, 4, lambda k: rest_line_copy(k).start())
-    second_step(MAIN_0)
     rest_last()
+    join_states()
     main_last(0)
+    add_line(1)
+    first_step(MAIN_1)
+    across(MAIN_0)
+    owner_rest()
     text_last()
     text_spread()
-    owner_main(0)
-    add_line(1)
-    first_step(MAIN_1)
-    owner_rest()
-    pack_main(0)
     second_step(MAIN_1)
-    across(MAIN_0)
-    pack_rest()
-    main_last(1)
-    text_spread_on()
-    spread(MAIN_0, main.at[OWN, 0])
+    spread(MAIN_0, OWN, 0)
     for copy in ways[0][:4]:
         copy.start()
-    owner_main(1)
-    across(REST_0)
-    across(REST_1)
     give(OWN, 0)
-    pack_main(1)
+    main_last(1)
+    pack_rest()
     ways[0][0].wait_recv()
     ways[0][4].start()
     ways[0][1].wait_recv()
     ways[0][5].start()
     across(MAIN_1)
-    for tile in range(2):
-        spread(REST_0 + tile, rest_w.at[tile])
-        give(REST, tile)
-    spread(MAIN_1, main.at[OWN, 1])
+    across(REST_0)
+    across(REST_1)
+    text_spread_on()
+    spread(MAIN_1, OWN, 1)
     for copy in ways[1][:4]:
         copy.start()
     give(OWN, 1)
-
+    ways[0][2].wait_recv()
+    give(LEFT, 0)
+    ways[0][3].wait_recv()
+    give(RIGHT, 0)
     for tile in range(2):
-        ways[tile][2].wait_recv()
-        give(LEFT, tile)
-        ways[tile][3].wait_recv()
-        give(RIGHT, tile)
-        if tile == 0:
-            ways[1][0].wait_recv()
-            ways[1][4].start()
-            ways[1][1].wait_recv()
-            ways[1][5].start()
-        ways[tile][4].wait_recv()
-        ways[tile][5].wait_recv()
-        give(OPP, tile)
-
+        spread(REST_0 + tile, REST, tile)
+        give(REST, tile)
+    ways[0][4].wait_recv()
+    ways[0][5].wait_recv()
+    give(OPP, 0)
+    ways[1][0].wait_recv()
+    ways[1][4].start()
+    ways[1][1].wait_recv()
+    ways[1][5].start()
+    owner_main(0)
+    owner_main(1)
     for r in range(10):
         for layer in range(2):
             vision_sum[r, layer : layer + 1, :] = dense[layer, r : r + 1, :]
+
     for role in order:
         pair(role).wait_send()
     for copy in line[0] + line[1]:
@@ -649,26 +635,28 @@
         loop(1, 4, lambda k: second_copy(part, k).wait_send())
         loop(1, 4, lambda k: plane1(part, k).wait_send())
         loop(1, 4, lambda k: plane2(part, k).wait_send())
-    loop(1, 4, lambda k: rest_line_copy(k).wait_send())
-    rest_win().wait_send()
+    loop(1, 8, lambda i: state_copy(i).wait_send())
+    loop(1, 8, lambda i: rest_win_copy(i).wait_send())
     for tile in range(2):
         loop(1, 8, lambda i: win_copy(tile, i).wait_send())
-        loop(1, 8, lambda i: line_copy(tile, i).wait_send())
     loop(1, 8, lambda i: line_rest_copy(i).wait_send())
     beside_copy().wait_send()
     loop(1, 4, lambda k: x_copy(k).wait_send())
+
+    ways[1][2].wait_recv()
+    give(LEFT, 1)
+    ways[1][3].wait_recv()
+    give(RIGHT, 1)
+    ways[1][4].wait_recv()
+    ways[1][5].wait_recv()
+    give(OPP, 1)
     loop(1, 4, lambda k: upper_on(k).wait())
     loop(0, 4, lambda px: lower_on(px).wait())
-    arrivals = [(OWN, 0), (REST, 0), (REST, 1), (OWN, 1), (LEFT, 0), (RIGHT, 0), (OPP, 0), (LEFT, 1), (RIGHT, 1), (OPP, 1)]
-    for role, tile in arrivals:
-        mate(role, tile).wait_recv()
-        write(role, tile, 1).start()
     for copy in ways[0] + ways[1]:
         copy.wait_send()
-    for role, tile in arrivals:
-        mate(role, tile).wait_send()
-        write(role, tile, 0).wait()
-        write(role, tile, 1).wait()
+    for role in range(5):
+        for tile in range(2):
+            mate(role, tile).wait()
 
 
 def kernel_of(given):
@@ -693,10 +681,10 @@
             jax.ShapeDtypeStruct((rows, COLS), F32),
             jax.ShapeDtypeStruct(vision_states[0].shape, F32),
             jax.ShapeDtypeStruct((rows, 8 * COLS), BF16),
-            jax.ShapeDtypeStruct((2, GROUPS, ROWS, 5 * COLS), BF16),
+            jax.ShapeDtypeStruct((2, 10) + tile, BF16),
         ),
         in_specs=[pl.BlockSpec(memory_space=pltpu.HBM)] * 8,
-        out_specs=[pl.BlockSpec(memory_space=pltpu.VMEM)] * 2 + [pl.BlockSpec(memory_space=pltpu.HBM)] * 2,
+        out_specs=[pl.BlockSpec(memory_space=pltpu.VMEM)] * 4,
         scratch_shapes=[
             vmem((5,) + block, BF16),
             vmem((5,) + block, BF16),
@@ -711,11 +699,10 @@
             vmem((4, 4, ROWS, TILE), BF16),
             vmem((4, 4, ROWS, TILE), BF16),
             vmem((4, 2) + tile, BF16),
-            vmem((2, ROWS, TILE), BF16),
-            vmem((4, 2, ROWS, TILE), BF16),
             vmem((2, ROWS, TILE), F32),
             vmem((2, ROWS, TILE), F32),
-            vmem((2, 10, 24, TILE), F32),
+            vmem((2, 8, 24, TILE), F32),
+            vmem((2, 4, 2, 24, TILE), F32),
             vmem((4, 2, half, COLS), BF16),
             vmem((4, half, COLS), BF16),
             vmem((4, half, COLS), BF16),
@@ -725,18 +712,15 @@
             vmem((4, half, COLS), BF16),
             vmem((3, rows, COLS), F32),
             vmem((3,) + vision_states[0].shape, F32),
-            vmem((3, 2, 16, 5 * COLS), F32),
+            vmem((2, 32, 5 * COLS), F32),
+            vmem((8, 32, COLS), F32),
+            vmem((3, ROWS, COLS), F32),
             vmem((2, 16, 5 * COLS), F32),
-            vmem((2, 2, 4, 16, TILE), BF16),
             vmem((2, 2, 16, TILE), BF16),
-            vmem((2, 8, 16, TILE), BF16),
             vmem((8, 2, 16, TILE), BF16),
-            vmem((4, ROWS, TILE), F32),
+            vmem((2, ROWS, TILE), F32),
             vmem((rows, COLS), BF16),
             vmem((4,) + square, BF16),
-            vmem((4, 2) + tile, BF16),
-            vmem((2,) + tile, BF16),
-            vmem((5, 2) + tile, BF16),
             dma((5, 2)),
             dma((6,)),
             dma((3, 2)),
@@ -744,18 +728,18 @@
             dma((2, 6)), dma((2, 6)),
             dma((4, 4)), dma((4, 4)),
             dma((4, 4)), dma((4, 4)),
-            dma((4,)), dma((4,)),
+            dma((8,)), dma((8,)),
             dma((2, 8)), dma((2, 8)),
+            dma((8,)), dma((8,)),
             dma((8, 2)), dma((8, 2)),
             dma((4,)), dma((4,)),
-            dma((3, 8)), dma((3, 8)),
+            dma((8,)), dma((8,)),
             dma((4, 4)), dma((4, 4)),
             dma((4, 4)), dma((4, 4)),
             dma((2, 6)), dma((2, 6)),
             dma((5, 2)), dma((5, 2)),
             dma((3, 4)), dma((3, 4)),
             dma,
-            dma((5, 2, 2)),
         ],
         compiler_params=pltpu.CompilerParams(collective_id=1, has_side_effects=True, vmem_limit_bytes=40 << 20),
     )(*[pltpu.with_memory_space_constraint(array, pltpu.HBM) for array in (text, vision, *text_states, *vision_states)])
@@ -764,12 +748,14 @@
 def finish_kernel(*refs):
     text, vision, text_full, vision_full = refs[:5], refs[5:10], refs[10], refs[11]
     outs, vision_w = refs[12:22], refs[21]
-    text_made, vision_made, sem = refs[22:]
+    text_made, vision_made, sem, tile_sem = refs[22:]
     text_w = outs[4]
     copies = [
-        pltpu.make_async_copy(vision_full, vision_w, sem.at[0]),
-        pltpu.make_async_copy(text_full, text_w, sem.at[1]),
+        pltpu.make_async_copy(vision_full.at[layer, t], vision_w.at[layer, :, :, t * TILE : (t + 1) * TILE], tile_sem.at[layer, t])
+        for layer in range(2)
+        for t in range(10)
     ]
+    copies.append(pltpu.make_async_copy(text_full, text_w, sem.at[1]))
     for copy in copies:
         copy.start()
 
@@ -805,13 +791,17 @@
     return pl.pallas_call(
         finish_kernel,
         name="write_results",
-        out_shape=(like(text[0]),) * 4 + (like(text_full),) + (like(vision[0]),) * 4 + (like(vision_full),),
+        out_shape=(like(text[0]),) * 4
+        + (like(text_full),)
+        + (like(vision[0]),) * 4
+        + (jax.ShapeDtypeStruct((2, GROUPS, ROWS, 5 * COLS), BF16),),
         in_specs=[in_vmem] * 10 + [in_hbm] * 2,
         out_specs=[in_hbm] * 10,
         scratch_shapes=[
             pltpu.VMEM((4,) + text[0].shape, F32),
             pltpu.VMEM((4,) + vision[0].shape, F32),
             pltpu.SemaphoreType.DMA((10,)),
+            pltpu.SemaphoreType.DMA((2, 10)),
         ],
         compiler_params=pltpu.CompilerParams(vmem_limit_bytes=16 << 20),
     )(*text, *vision, text_full, vision_full)

time: 96.6 us -> 80.6 us (0.83)
  Pallas kernels: 95.7 us -> 79.7 us
    pallas_call x1, Pallas kernels: 91.5 us -> 75.3 us  [step(): pl.pallas_call(kernel_of(step_kernel), name='sum_step_gather', out_shape=...]
where the time goes in v4:
time: 80.6 us; the launch traced here: 80.5 us
  Pallas kernels  79.7 us (99%)
    pallas_call x1, Pallas kernels, step(): pl.pallas_call(kernel_of(step_kernel), name='sum_step_gather', out_shape=...  75.3 us
    pallas_call x1, Pallas kernels, finish(): pl.pallas_call(finish_kernel, name='write_results', out_shape=(like(text[...  4.36 us

profile of v4, /device:TPU:1, one launch (start us, length us, event | category | flops | bytes accessed | tf_op | source)
XLA Modules:
  0.0 80.5 jit_solution(5129153558079707037)
XLA Ops:
  0.6 0.0 copy-start.1
  0.7 0.0 copy-start
  0.7 0.0 copy-start.2
  0.7 0.0 copy-start.7
  0.7 0.0 copy-start.5
  0.7 0.0 copy-start.4
  0.7 0.0 copy-start.6
  0.7 0.0 copy-start.3
  0.7 75.3 %sum_step_gather.1 = (f32[512,256]{1,0:T(8,128)S(1)}, f32[10,2,1280]{2,1,0:T(2,128)S(1)}, bf16[512,2048]{1,0:T(8,128)(2,1)S(1)}, bf16[2,10,16,80,128]{4,3,2,1,0:T(8,128)(2,1)S(1)}) custom-call(bf16[512,2048]{1,0:T(8,128)(2,1)} %bitcast.19, bf16[2,16,80,1280]{3,2,1,0:T(8,128)(2,1)} %bitcast.18, f32[512,256]{1,0:T(8,128)} %refs_1_.3, f32[512,256]{1,0:T(8,128)} %refs_2_.3, ...), custom_call_target="tpu_custom_call" | custom-call | tf_op jit(solution)/shard_map/sum_step_gather/pallas_call | solution.py:677
  76.1 0.0 copy-done.1
  76.1 0.0 copy-done
  76.1 0.0 copy-done.2
  76.1 0.0 copy-done.7
  76.1 0.0 copy-done.5
  76.1 0.0 copy-done.4
  76.1 0.0 copy-done.6
  76.1 0.0 copy-done.3
  76.2 4.4 %write_results.1 = (f32[512,256]{1,0:T(8,128)}, f32[512,256]{1,0:T(8,128)}, f32[512,256]{1,0:T(8,128)}, f32[512,256]{1,0:T(8,128)}, bf16[512,2048]{1,0:T(8,128)(...) custom-call(f32[512,256]{1,0:T(8,128)S(1)} %get-tuple-element.24.ref, ...), custom_call_target="tpu_custom_call" | custom-call | tf_op jit(solution)/shard_map/write_results/pallas_call | solution.py:791
Async XLA Ops:
  0.6 75.4 %copy-start.1 = (f32[512,256]{1,0:T(8,128)S(1)}, f32[512,256]{1,0:T(8,128)}, u32[]{:S(2)}) copy-start(f32[512,256]{1,0:T(8,128)} %refs_2_.3) | copy-start | bytes 1572868
  0.7 75.4 %copy-start = (f32[512,256]{1,0:T(8,128)S(1)}, f32[512,256]{1,0:T(8,128)}, u32[]{:S(2)}) copy-start(f32[512,256]{1,0:T(8,128)} %refs_1_.3) | copy-start | bytes 1572868
  0.7 75.4 %copy-start.2 = (f32[512,256]{1,0:T(8,128)S(1)}, f32[512,256]{1,0:T(8,128)}, u32[]{:S(2)}) copy-start(f32[512,256]{1,0:T(8,128)} %refs_3_.1) | copy-start | bytes 1572868
  0.7 75.4 %copy-start.7 = (f32[2,10,1280]{2,0,1:T(2,128)S(1)}, f32[2,10,1280]{2,0,1:T(2,128)}, u32[]{:S(2)}) copy-start(f32[2,10,1280]{2,0,1:T(2,128)} %param.19) | copy-start | bytes 307204
  0.7 75.4 %copy-start.5 = (f32[2,10,1280]{2,0,1:T(2,128)S(1)}, f32[2,10,1280]{2,0,1:T(2,128)}, u32[]{:S(2)}) copy-start(f32[2,10,1280]{2,0,1:T(2,128)} %param.18) | copy-start | bytes 307204
  0.7 75.4 %copy-start.4 = (f32[2,10,1280]{2,0,1:T(2,128)S(1)}, f32[2,10,1280]{2,0,1:T(2,128)}, u32[]{:S(2)}) copy-start(f32[2,10,1280]{2,0,1:T(2,128)} %param.17) | copy-start | bytes 307204
  0.7 75.4 %copy-start.6 = (f32[2,10,1280]{2,0,1:T(2,128)S(1)}, f32[2,10,1280]{2,0,1:T(2,128)}, u32[]{:S(2)}) copy-start(f32[2,10,1280]{2,0,1:T(2,128)} %param.16) | copy-start | bytes 307204
  0.7 75.4 %copy-start.3 = (f32[512,256]{1,0:T(8,128)S(1)}, f32[512,256]{1,0:T(8,128)}, u32[]{:S(2)}) copy-start(f32[512,256]{1,0:T(8,128)} %refs_4_.1) | copy-start | bytes 1572868

commit v5 on v4

v5 whole, which is shorter than its diff:
```python
import functools

import jax
import jax.numpy as jnp
from jax import lax
from jax.experimental import pallas as pl
from jax.experimental.pallas import tpu as pltpu
from jax.sharding import PartitionSpec as P

MESH = pl.DeviceIdType.MESH
BF16, F32 = jnp.bfloat16, jnp.float32

beta_one = 0.9
beta_two = 0.95
correct_one = 1.0 - 0.9**10
correct_two = 1.0 - 0.95**10
learn_rate = 0.01
decay_rate = 0.1
blend_rate = 0.6

GROUPS = 16
ROWS = 80
TILE = 128
UPPER = 9
COLS = 2 * TILE
OPP, RIGHT, LEFT, OWN, REST = range(5)
PIECES = ((0, 0, 32), (0, 32, 48), (1, 0, 48), (1, 48, 32))
UNITS = ((0, 0, 2 * ROWS),) + tuple((1 + tile, first, n) for tile, first, n in PIECES)


def adam_step(grad, moment, second, master, refcopy):
    moment_new = beta_one * moment + (1.0 - beta_one) * grad
    second_new = beta_two * second + (1.0 - beta_two) * grad * grad
    update = moment_new / correct_one / (jnp.sqrt(second_new / correct_two) + 1e-08)
    master_new = master - learn_rate * (update + decay_rate * master)
    ref_new = blend_rate * master_new + (1.0 - blend_rate) * refcopy
    return (master_new, moment_new, second_new, ref_new, master_new.astype(BF16))


def adam_weights(grad, moment, second, master):
    return adam_step(grad, moment, second, master, master)[4]


def place():
    dp, tensor = lax.axis_index("dp"), lax.axis_index("tensor")
    x = dp // 2
    z = (tensor // 8) * 2 + dp % 2
    y = (tensor % 8) // 2
    return x, y, z, tensor % 2


def device(x, y, z, core):
    return (x * 2 + z % 2, (z // 2) * 8 + y * 2 + core)


def group_of(x, z):
    return x * 4 + (z % 2) * 2 + z // 2


def first_row(y):
    return pl.multiple_of(8 * ((5 * y) // 2), 8)


def columns(block, width):
    return pl.ds(pl.multiple_of(block * width, width), width)


def remote(src, dst, send, recv, to):
    return pltpu.make_async_remote_copy(
        src_ref=src, dst_ref=dst, send_sem=send, recv_sem=recv, device_id=to, device_id_type=MESH
    )


def loop(first, last, step):
    def run(i, carry):
        step(i)
        return carry

    lax.fori_loop(first, last, run, 0)


def each(first, last, step):
    for i in range(first, last):
        step(i)


class Near:
    def __init__(self):
        self.x, self.y, self.z, self.core = place()
        x, y, z, core = self.x, self.y, self.z, self.core
        self.dp = x * 2 + z % 2
        self.twin = z % 2
        self.a = x * (1 - core) + z * core
        self.b = x * core + z * (1 - core)
        self.mate = device(x, y, z, 1 - core)
        self.beside = device(x, y, z + 1 - 2 * (z % 2), core)
        xs, ys, zs = ([(at + k) % 4 for k in range(4)] for at in (x, y, z))
        self.xs = xs
        self.a_at = [jnp.where(core == 0, xs[k], zs[k]) for k in range(4)]
        self.b_at = [jnp.where(core == 0, zs[k], xs[k]) for k in range(4)]
        self.along_x = [device(xs[k], y, z, core) for k in range(4)]
        along_z = [device(x, y, zs[k], core) for k in range(4)]
        self.along_y = [device(x, ys[k], z, core) for k in range(4)]
        self.right, self.left = self.along_y[1], self.along_y[3]

        def choose(first, second):
            return [tuple(jnp.where(core == 0, p, q) for p, q in zip(one, two)) for one, two in zip(first, second)]

        self.along_a = choose(self.along_x, along_z)
        self.along_b = choose(along_z, self.along_x)
        other = [device(x, ys[k], z, 1 - core) for k in range(4)]
        self.line = [((self.along_y, other)[i % 2][i // 2], ys[i // 2], (core, 1 - core)[i % 2]) for i in range(8)]

    def group(self, a, b):
        return jnp.where(self.core == 0, a * 4 + (b % 2) * 2 + b // 2, b * 4 + (a % 2) * 2 + a // 2)

    def greet(self):
        barrier = pltpu.get_barrier_semaphore()

        def signal(to):
            pl.semaphore_signal(barrier, inc=1, device_id=to, device_id_type=MESH)

        each(1, 4, lambda k: signal(self.along_a[k]))
        each(1, 4, lambda k: signal(self.along_b[k]))
        each(1, 8, lambda i: signal(self.line[i][0]))

    def meet(self):
        pl.semaphore_wait(pltpu.get_barrier_semaphore(), 13)


def step_kernel(
    text_hbm, vision_hbm, text_states, vision_states, text_sum, vision_sum, text_out, vision_out,
    mine, other, paired, over_a, over_b, from_left, from_right, total, rest, first_in, first_sum, second_in, first_in_rest,
    first_sum_rest, second_in_rest, plane_rest, reduced,
    sums, rest_sums, windows, rest_windows, upper_own, upper_mid, upper_over, upper_from, lower_own, lower_in, lower_sum, cross_out, cross_in, lower_x,
    text_state, vision_raw, own_state, line_state, tile_state, dense, staged_rest, line_rest, packed, text_w, plane,
    load_sem, text_load, state_load, pair_s, pair_r, y_s, y_r, first_s, first_r, second_s, second_r,
    state_s, state_r, win_s, win_r, rest_win_s, rest_win_r, upper_s, upper_r, text_s, text_r, text2_s, text2_r,
    line_s, line_r, plane1_s, plane1_r, plane2_s, plane2_r, back_s, back_r, mate_s, mate_r, spread_s, spread_r,
    own_sem,
):
    near = Near()
    x, y, core = near.x, near.y, near.core
    up = UPPER * text_hbm.shape[0] // 16
    low = text_hbm.shape[0] - up
    upper_rows, lower_rows = pl.ds(0, up), pl.ds(up, low)
    blocks = [(y + 2) % 4, (y + 1) % 4, (y + 3) % 4, y, 4]
    order = (OPP, RIGHT, LEFT, REST, OWN)

    def loads(role):
        cols = columns(blocks[role], COLS)
        return (
            pltpu.make_async_copy(vision_hbm.at[1 - core, :, :, cols], other.at[role], load_sem.at[role, 0]),
            pltpu.make_async_copy(vision_hbm.at[core, :, :, cols], mine.at[role], load_sem.at[role, 1]),
        )

    def text_block(rows, block):
        return text_hbm.at[rows, columns(block, COLS)]

    def upper_load(q):
        return pltpu.make_async_copy(text_block(upper_rows, 2 * x + q), upper_own.at[q], text_load.at[q])

    def mid_load(q):
        return pltpu.make_async_copy(text_block(upper_rows, 2 * near.xs[1 + 2 * q] + q), upper_mid.at[q], text_load.at[6 + q])

    def lower_load(px):
        return pltpu.make_async_copy(text_block(lower_rows, 2 * px + near.twin), lower_own.at[px], text_load.at[2 + px])

    def state_copies(i):
        return (
            pltpu.make_async_copy(text_states[i], text_state.at[i], state_load.at[i, 0]),
            pltpu.make_async_copy(vision_states[i], vision_raw.at[i], state_load.at[i, 1]),
        )

    near.greet()
    for copy in loads(OPP):
        copy.start()
    for i in range(3):
        state_copies(i)[1].start()
    for role in order[1:]:
        for copy in loads(role):
            copy.start()
    each(0, 2, lambda q: upper_load(q).start())
    each(0, 2, lambda q: mid_load(q).start())
    each(0, 4, lambda px: lower_load(px).start())
    for i in range(3):
        state_copies(i)[0].start()

    near.meet()

    ahead, behind = near.along_x[1], near.along_x[3]

    def upper_copies():
        def go(src, dst, i, to):
            return remote(src, dst, upper_s.at[i], upper_r.at[i], to)

        def block(k, q):
            return text_block(upper_rows, 2 * near.xs[k] + q)

        return [
            go(block(2, 0), upper_over.at[0], 0, ahead),
            go(block(2, 1), upper_over.at[1], 1, behind),
            go(block(1, 1), upper_from.at[0, 1], 2, ahead),
            go(block(3, 0), upper_from.at[1, 0], 3, behind),
            go(upper_mid.at[0], upper_from.at[0, 0], 4, ahead),
            go(upper_mid.at[1], upper_from.at[1, 1], 5, behind),
        ]

    upper = upper_copies()

    def text_pass_on():
        each(0, 2, lambda q: mid_load(q).wait())
        for q in range(2):
            upper[q].wait_recv()

            def add(i, q=q):
                rows = pl.ds(pl.multiple_of(i * 32, 32), 32)
                upper_mid[q, rows] = upper_mid[q, rows] + upper_over[q, rows]

            loop(0, up // 32, add)
            upper[4 + q].start()

    def lower_copy(px):
        return remote(
            text_block(lower_rows, 2 * px + 1 - near.twin), lower_in.at[px], text_s.at[px], text_r.at[px],
            near.beside,
        )

    def pair(role, tile=None):
        cols = pl.ds(0, COLS) if tile is None else pl.ds(tile * TILE, TILE)
        src, dst = other.at[role, :, :, cols], paired.at[role, :, :, cols]
        return remote(src, dst, pair_s.at[role, tile or 0], pair_r.at[role, tile or 0], near.mate)

    def add_pair(role, tile):
        if tile == 0:
            loads(role)[1].wait()
        pair(role, tile).wait_recv()
        cols = slice(tile * TILE, (tile + 1) * TILE)

        def add(i):
            for j in range(4):
                g = 4 * i + j
                reduced[role, tile, g] = mine[role, g, :, cols] + paired[role, g, :, cols]

        loop(0, GROUPS // 4, add)

    def add_own():
        loads(OWN)[1].wait()
        pair(OWN).wait_recv()

        def add(i):
            for j in range(4):
                g = 4 * i + j
                both = mine[OWN, g] + paired[OWN, g]
                reduced[OWN, 0, g] = both[:, :TILE]
                reduced[OWN, 1, g] = both[:, TILE:]

        loop(0, GROUPS // 4, add)

    def add_rest():
        loads(REST)[1].wait()
        pair(REST).wait_recv()

        def add(i):
            a, b = i // 4, i % 4
            g = near.group(a, b)
            both = mine[REST, g] + paired[REST, g]
            rest[a, b, :ROWS] = both[:, :TILE]
            rest[a, b, ROWS:] = both[:, TILE:]

        each(0, GROUPS, add)

    half_a, half_b = pl.ds(0, 8), pl.ds(8, 8)

    def along(piece):
        tile, first, n = PIECES[piece]
        rows = pl.ds(first, n)

        def go(src, dst, i, to):
            return remote(src, dst, y_s.at[piece, i], y_r.at[piece, i], to)

        return [
            go(reduced.at[OPP, tile, half_a, rows], over_a.at[tile, :, rows], 0, near.right),
            go(reduced.at[OPP, tile, half_b, rows], over_b.at[tile, :, rows], 1, near.left),
            go(reduced.at[RIGHT, tile, half_b, rows], from_left.at[tile, half_b, rows], 2, near.right),
            go(reduced.at[LEFT, tile, half_a, rows], from_right.at[tile, half_a, rows], 3, near.left),
            go(reduced.at[RIGHT, tile, half_a, rows], from_left.at[tile, half_a, rows], 4, near.right),
            go(reduced.at[LEFT, tile, half_b, rows], from_right.at[tile, half_b, rows], 5, near.left),
        ]

    line = [along(piece) for piece in range(len(PIECES))]

    def pass_on(piece):
        tile, first, n = PIECES[piece]
        rows = pl.ds(first, n)
        line[piece][0].wait_recv()

        def add_a(i):
            for g in (2 * i, 2 * i + 1):
                reduced[RIGHT, tile, g, rows] = reduced[RIGHT, tile, g, rows] + over_a[tile, g, rows]

        loop(0, 4, add_a)
        line[piece][4].start()
        line[piece][1].wait_recv()

        def add_b(i):
            for g in (2 * i, 2 * i + 1):
                reduced[LEFT, tile, 8 + g, rows] = reduced[LEFT, tile, 8 + g, rows] + over_b[tile, g, rows]

        loop(0, 4, add_b)
        line[piece][5].start()

    def add_line(piece):
        tile, first, n = PIECES[piece]
        rows = pl.ds(first, n)
        for copy in line[piece][2:]:
            copy.wait_recv()

        def add(i):
            a, b = i // 4, i % 4
            g = near.group(a, b)
            total[tile, a, b, rows] = (
                reduced[OWN, tile, g, rows].astype(F32)
                + from_left[tile, g, rows].astype(F32)
                + from_right[tile, g, rows].astype(F32)
            ).astype(BF16)

        each(0, GROUPS, add)

    def pick(unit, of_rest, of_main):
        buffer, first, n = UNITS[unit]
        return of_rest if buffer == 0 else of_main.at[buffer - 1], pl.ds(first, n)

    def source(unit, a):
        ref, rows = pick(unit, rest, total)
        return ref.at[a, :, rows]

    def first_copy(unit, k):
        ref, rows = pick(unit, first_in_rest, first_in)
        return remote(
            source(unit, near.a_at[k]), ref.at[k, :, rows], first_s.at[unit, k], first_r.at[unit, k], near.along_a[k]
        )

    def second_copy(unit, k):
        src, rows = pick(unit, first_sum_rest, first_sum)
        dst, _ = pick(unit, second_in_rest, second_in)
        return remote(
            src.at[near.b_at[k], rows], dst.at[k, rows], second_s.at[unit, k], second_r.at[unit, k], near.along_b[k]
        )

    def first_step(unit):
        each(1, 4, lambda k: first_copy(unit, k).start())

    def second_step(unit):
        each(1, 4, lambda k: first_copy(unit, k).wait_recv())
        own = source(unit, near.a)
        got, rows = pick(unit, first_in_rest, first_in)
        made, _ = pick(unit, first_sum_rest, first_sum)

        def add(b):
            acc = own[b].astype(F32)
            for k in range(1, 4):
                acc = acc + got[k, b, rows].astype(F32)
            made[b, rows] = acc.astype(BF16)

        each(0, 4, add)
        each(1, 4, lambda k: second_copy(unit, k).start())

    def last_step(unit):
        each(1, 4, lambda k: second_copy(unit, k).wait_recv())
        made, rows = pick(unit, first_sum_rest, first_sum)
        got, _ = pick(unit, second_in_rest, second_in)
        acc = made[near.b, rows].astype(F32)
        for k in range(1, 4):
            acc = acc + got[k, rows].astype(F32)
        return acc

    def cross_copy():
        return remote(cross_out, cross_in, text2_s.at[0], text2_r.at[0], near.beside)

    def lower_x_copy(k):
        return remote(
            lower_sum.at[near.xs[k]], lower_x.at[k], text2_s.at[k], text2_r.at[k], near.along_x[k]
        )

    def text_middle():
        each(0, 2, lambda q: upper_load(q).wait())
        for copy in upper[2:]:
            copy.wait_recv()

        def add_upper(i):
            rows = pl.ds(pl.multiple_of(i * 32, 32), 32)

            def both(q):
                return upper_own[q, rows].astype(F32) + upper_from[0, q, rows].astype(F32) + upper_from[1, q, rows].astype(F32)

            cross_out[rows] = both(1 - near.twin).astype(BF16)
            text_sum[rows] = both(near.twin)

        loop(0, up // 32, add_upper)
        each(0, 4, lambda px: lower_load(px).wait())
        each(0, 4, lambda px: lower_copy(px).wait_recv())

        def add_lower(i):
            rows = pl.ds(pl.multiple_of(i * 32, 32), 32)
            for px in range(4):
                lower_sum[px, rows] = lower_own[px, rows] + lower_in[px, rows]

        loop(0, low // 32, add_lower)

    def text_cross():
        cross_copy().start()
        lower_x_copy(1).start()
        lower_x_copy(3).start()

    def text_weights(rows, grad):
        text_sum[rows] = grad
        text_w[rows] = adam_weights(grad, *[text_state[i, rows] for i in range(3)])

    def text_last():
        for i in range(3):
            state_copies(i)[0].wait()
        cross_copy().wait_recv()
        each(1, 4, lambda k: lower_x_copy(k).wait_recv())

        def add(i):
            rows = pl.ds(pl.multiple_of(i * 32, 32), 32)
            text_weights(rows, text_sum[rows] + cross_in[rows].astype(F32))

        def add_low(i):
            rows = pl.ds(pl.multiple_of(i * 32, 32), 32)
            acc = lower_own[x, rows].astype(F32) + lower_in[x, rows].astype(F32)
            for k in range(1, 4):
                acc = acc + lower_x[k, rows].astype(F32)
            text_weights(pl.ds(pl.multiple_of(up + i * 32, 32), 32), acc)

        loop(0, up // 32, add)
        loop(0, low // 32, add_low)

    def arrange_states():
        for i in range(3):
            state_copies(i)[1].wait()
        for layer in range(2):
            for i in range(3):
                for r in range(10):
                    own_state[layer, 10 * i + r : 10 * i + r + 1, :] = vision_raw[i, r, layer : layer + 1, :]

    def state_copy(i):
        to, py, pc = near.line[i]
        return remote(
            own_state.at[pc, :, columns(py, COLS)], line_state.at[y * 2 + core], state_s.at[i], state_r.at[i], to
        )

    def send_states():
        each(1, 8, lambda i: state_copy(i).start())
        line_state[y * 2 + core] = own_state[core, :, columns(y, COLS)]

    def join_states():
        each(1, 8, lambda i: state_copy(i).wait_recv())
        for place_on_line in range(8):
            for i in range(3):
                tile_state[i, 10 * place_on_line : 10 * place_on_line + 10, :] = line_state[
                    place_on_line, 10 * i : 10 * i + 10, :
                ]

    own_rows = pl.ds(first_row(y), 24)

    def win_copy(tile, i):
        to, py, _ = near.line[i]
        return remote(
            sums.at[tile, pl.ds(first_row(py), 24)], windows.at[core, 2 * y + tile], win_s.at[tile, i], win_r.at[tile, i],
            to,
        )

    def rest_win_copy(i):
        to, py, _ = near.line[i]
        return remote(
            rest_sums.at[:, pl.ds(first_row(py), 24)], rest_windows.at[core, y], rest_win_s.at[i], rest_win_r.at[i], to
        )

    def main_last(piece):
        tile, first, n = PIECES[piece]
        rows = pl.ds(first, n)
        grad = last_step(1 + piece)
        sums[tile, rows] = grad
        cols = slice(tile * TILE, (tile + 1) * TILE)
        plane[tile, near.a, near.b, rows] = adam_weights(grad, *[tile_state[i, rows, cols] for i in range(3)])
        each(1, 4, lambda k: plane1(1 + piece, k).start())

    def send_sums(tile):
        each(1, 8, lambda i: win_copy(tile, i).start())
        windows[core, 2 * y + tile] = sums[tile, own_rows]

    def rest_last():
        both = last_step(0)
        rest_sums[0] = both[:ROWS]
        rest_sums[1] = both[ROWS:]
        each(1, 8, lambda i: rest_win_copy(i).start())
        rest_windows[core, y] = rest_sums[:, own_rows]

    odd = y % 2 == 1

    def own_part(window):
        first = jnp.where(odd, window[4:14], window[0:10])
        second = jnp.where(odd, window[14:24], window[10:20])
        return jnp.where(core == 1, second, first)

    def line_rest_copy(i):
        to, _, pc = near.line[i]
        return remote(staged_rest.at[pc], line_rest.at[y * 2 + core], line_s.at[i], line_r.at[i], to)

    def owner_rest():
        each(1, 8, lambda i: rest_win_copy(i).wait_recv())
        for layer in range(2):
            for tile in range(2):
                cols = slice((8 + tile) * TILE, (9 + tile) * TILE)
                window = rest_windows[layer, 0, tile]
                for py in range(1, 4):
                    window = window + rest_windows[layer, py, tile]
                grad = own_part(window)
                dense[layer, 0:10, cols] = grad
                staged_rest[layer, tile, 0:10] = adam_weights(
                    grad, *[own_state[layer, 10 * i : 10 * i + 10, cols] for i in range(3)]
                )
        each(1, 8, lambda i: line_rest_copy(i).start())
        line_rest[y * 2 + core] = staged_rest[core]

    def owner_main(tile):
        each(1, 8, lambda i: win_copy(tile, i).wait_recv())
        for layer in range(2):
            for py in range(4):
                t = 2 * py + tile
                dense[layer, 0:10, t * TILE : (t + 1) * TILE] = own_part(windows[layer, t])

    def plane1(unit, k):
        ref, rows = pick(unit, plane_rest, plane)
        one = ref.at[near.a, near.b, rows]
        return remote(one, one, plane1_s.at[unit, k], plane1_r.at[unit, k], near.along_b[k])

    def plane2(unit, k):
        ref, rows = pick(unit, plane_rest, plane)
        row = ref.at[near.a, :, rows]
        return remote(row, row, plane2_s.at[unit, k], plane2_r.at[unit, k], near.along_a[k])

    def pack_rest():
        each(1, 8, lambda i: line_rest_copy(i).wait_recv())
        for tile in range(2):
            for i in range(8):
                packed[tile, 10 * i : 10 * i + 10, :] = line_rest[i, tile].astype(F32)[:10]
            plane_rest[near.a, near.b, tile * ROWS : (tile + 1) * ROWS] = packed[tile].astype(BF16)
        each(1, 4, lambda k: plane1(0, k).start())

    def across(unit):
        each(1, 4, lambda k: plane1(unit, k).wait_recv())
        each(1, 4, lambda k: plane2(unit, k).start())

    first_tile = {OPP: 2 * blocks[OPP], RIGHT: 2 * blocks[RIGHT], LEFT: 2 * blocks[LEFT], OWN: 2 * y, REST: 8}

    def held(role, tile):
        return vision_out.at[core, first_tile[role] + tile]

    def spread(unit):
        each(1, 4, lambda k: plane2(unit, k).wait_recv())
        buffer, first, n = UNITS[unit]
        rows = pl.ds(first, n)

        def move(i):
            a, b = i // 4, i % 4
            g = near.group(a, b)
            if buffer:
                vision_out[core, 2 * y + buffer - 1, g, rows] = plane[buffer - 1, a, b, rows]
            else:
                vision_out[core, 8, g] = plane_rest[a, b, :ROWS]
                vision_out[core, 9, g] = plane_rest[a, b, ROWS:]

        each(0, GROUPS, move)

    def back(piece):
        tile, first, n = PIECES[piece]
        rows = pl.ds(first, n)

        def go(role, half, i, to):
            part = held(role, tile).at[half, rows]
            return remote(part, part, back_s.at[piece, i], back_r.at[piece, i], to)

        nearer = [
            go(OWN, half_a, 0, near.right),
            go(OWN, half_b, 1, near.left),
            go(OWN, half_b, 2, near.right),
            go(OWN, half_a, 3, near.left),
        ]
        return nearer + [go(LEFT, half_a, 4, near.right), go(RIGHT, half_b, 5, near.left)]

    last = len(PIECES) - 1
    ways = [back(piece) for piece in range(len(PIECES))]

    def send_back(piece):
        spread(1 + piece)
        for copy in ways[piece][:4]:
            copy.start()
        give(OWN, piece)

    def forward(piece):
        ways[piece][0].wait_recv()
        ways[piece][4].start()
        ways[piece][1].wait_recv()
        ways[piece][5].start()

    def give_sides(piece):
        ways[piece][2].wait_recv()
        give(LEFT, piece)
        ways[piece][3].wait_recv()
        give(RIGHT, piece)

    def give_last(piece):
        ways[piece][4].wait_recv()
        ways[piece][5].wait_recv()
        give(OPP, piece)

    def mate(role, piece):
        if role == REST:
            part = held(role, piece)
        else:
            tile, first, n = PIECES[piece]
            part = held(role, tile).at[:, pl.ds(first, n)]
        return remote(part, part, mate_s.at[role, piece], mate_r.at[role, piece], near.mate)

    def give(role, piece):
        mate(role, piece).start()

    own_cols = columns(near.dp, COLS)

    def own_text():
        return pltpu.make_async_copy(text_w, text_out.at[:, own_cols], own_sem)

    def beside_copy():
        return remote(
            text_w.at[upper_rows], text_out.at[upper_rows, own_cols], spread_s.at[0, 0], spread_r.at[0, 0], near.beside
        )

    def x_copy(k):
        return remote(
            text_w.at[lower_rows], text_out.at[lower_rows, own_cols], spread_s.at[0, k], spread_r.at[0, k],
            near.along_x[k],
        )

    def upper_ways():
        def go(block, i, to):
            part = text_out.at[upper_rows, columns(block, COLS)]
            return remote(part, part, spread_s.at[1, i], spread_r.at[1, i], to)

        return [
            go(2 * x, 0, ahead),
            go(2 * x + 1, 1, behind),
            go(2 * x + 1, 2, ahead),
            go(2 * x, 3, behind),
            go(2 * near.xs[3], 4, ahead),
            go(2 * near.xs[1] + 1, 5, behind),
        ]

    upper_on = upper_ways()

    def text_spread_last():
        for i in range(2):
            upper_on[i].wait_recv()
            upper_on[4 + i].start()

    def lower_on(px):
        one = text_out.at[lower_rows, columns(2 * px + near.twin, COLS)]
        return remote(one, one, spread_s.at[2, px], spread_r.at[2, px], near.beside)

    def text_spread():
        own_text().start()
        beside_copy().start()
        x_copy(1).start()
        x_copy(3).start()

    def text_spread_on():
        own_text().wait()
        beside_copy().wait_recv()
        for copy in upper_on[:4]:
            copy.start()
        each(1, 4, lambda k: x_copy(k).wait_recv())
        each(0, 4, lambda px: lower_on(px).start())

    def start_pair(role, tile=None):
        if not tile:
            loads(role)[0].wait()
        pair(role, tile).start()

    start_pair(OPP, 0)
    start_pair(RIGHT, 0)
    add_pair(OPP, 0)
    line[0][0].start()
    line[0][1].start()
    start_pair(LEFT, 0)
    for copy in upper[:4]:
        copy.start()
    each(0, 4, lambda px: lower_copy(px).start())
    add_pair(RIGHT, 0)
    line[0][2].start()
    line[1][0].start()
    start_pair(REST)
    add_pair(LEFT, 0)
    line[0][3].start()
    line[1][1].start()
    start_pair(OWN)
    for role in (OPP, RIGHT, LEFT):
        start_pair(role, 1)
    add_rest()
    first_step(0)
    pass_on(0)
    line[1][2].start()
    line[1][3].start()
    add_own()
    arrange_states()
    text_pass_on()
    pass_on(1)
    send_states()
    for role in (OPP, RIGHT, LEFT):
        add_pair(role, 1)
    for copy in line[2][:4] + line[3][:4]:
        copy.start()
    add_line(0)
    first_step(1)
    text_middle()
    add_line(1)
    first_step(2)
    second_step(1)
    text_cross()
    pass_on(2)
    second_step(0)
    second_step(2)
    lower_x_copy(2).start()
    join_states()
    main_last(0)
    pass_on(3)
    rest_last()
    main_last(1)
    across(1)
    send_sums(0)
    add_line(2)
    first_step(3)
    across(2)
    owner_rest()
    send_back(0)
    add_line(3)
    first_step(4)
    second_step(3)
    text_last()
    text_spread()
    send_back(1)
    forward(0)
    second_step(4)
    x_copy(2).start()
    main_last(2)
    pack_rest()
    main_last(3)
    across(3)
    forward(1)
    across(4)
    across(0)
    send_back(2)
    text_spread_on()
    send_back(3)
    send_sums(1)
    give_sides(0)
    give_last(0)
    give_sides(1)
    give_last(1)
    forward(2)
    forward(3)
    text_spread_last()
    spread(0)
    give(REST, 0)
    give(REST, 1)
    give_sides(2)
    give_last(2)
    owner_main(0)
    owner_main(1)
    for r in range(10):
        for layer in range(2):
            vision_sum[r, layer : layer + 1, :] = dense[layer, r : r + 1, :]

    for role in (OPP, RIGHT, LEFT):
        for tile in range(2):
            pair(role, tile).wait_send()
    for role in (REST, OWN):
        pair(role).wait_send()
    for copies in line:
        for copy in copies:
            copy.wait_send()
    for copy in upper:
        copy.wait_send()
    each(0, 4, lambda px: lower_copy(px).wait_send())
    cross_copy().wait_send()
    each(1, 4, lambda k: lower_x_copy(k).wait_send())
    for unit in range(len(UNITS)):
        for copies in (first_copy, second_copy, plane1, plane2):
            each(1, 4, lambda k: copies(unit, k).wait_send())
    each(1, 8, lambda i: state_copy(i).wait_send())
    each(1, 8, lambda i: rest_win_copy(i).wait_send())
    for tile in range(2):
        each(1, 8, lambda i: win_copy(tile, i).wait_send())
    each(1, 8, lambda i: line_rest_copy(i).wait_send())
    beside_copy().wait_send()
    each(1, 4, lambda k: x_copy(k).wait_send())

    give_sides(3)
    give_last(3)
    for copy in upper_on[2:]:
        copy.wait_recv()
    for copy in upper_on:
        copy.wait_send()
    each(0, 4, lambda px: lower_on(px).wait())
    for copies in ways:
        for copy in copies:
            copy.wait_send()
    for role in range(5):
        for piece in range(2 if role == REST else len(PIECES)):
            mate(role, piece).wait()


def kernel_of(given):
    def run(text_hbm, vision_hbm, *refs):
        given(text_hbm, vision_hbm, refs[:3], refs[3:6], *refs[6:])

    return run


def step(text, vision, text_states, vision_states):
    rows = text.shape[0]
    up = UPPER * rows // 16
    low = rows - up
    block = (GROUPS, ROWS, COLS)
    tile = (GROUPS, ROWS, TILE)
    square = (4, 4, ROWS, TILE)
    dma = pltpu.SemaphoreType.DMA
    vmem = pltpu.VMEM
    return pl.pallas_call(
        kernel_of(step_kernel),
        name="sum_step_gather",
        out_shape=(
            jax.ShapeDtypeStruct((rows, COLS), F32),
            jax.ShapeDtypeStruct(vision_states[0].shape, F32),
            jax.ShapeDtypeStruct((rows, 8 * COLS), BF16),
            jax.ShapeDtypeStruct((2, 10) + tile, BF16),
        ),
        in_specs=[pl.BlockSpec(memory_space=pltpu.HBM)] * 8,
        out_specs=[pl.BlockSpec(memory_space=pltpu.VMEM)] * 4,
        scratch_shapes=[
            vmem((5,) + block, BF16),
            vmem((5,) + block, BF16),
            vmem((5,) + block, BF16),
            vmem((2, 8, ROWS, TILE), BF16),
            vmem((2, 8, ROWS, TILE), BF16),
            vmem((2,) + tile, BF16),
            vmem((2,) + tile, BF16),
            vmem((2,) + square, BF16),
            vmem((4, 4, 2 * ROWS, TILE), BF16),
            vmem((2,) + square, BF16),
            vmem((2, 4, ROWS, TILE), BF16),
            vmem((2, 4, ROWS, TILE), BF16),
            vmem((4, 4, 2 * ROWS, TILE), BF16),
            vmem((4, 2 * ROWS, TILE), BF16),
            vmem((4, 2 * ROWS, TILE), BF16),
            vmem((4, 4, 2 * ROWS, TILE), BF16),
            vmem((4, 2) + tile, BF16),
            vmem((2, ROWS, TILE), F32),
            vmem((2, ROWS, TILE), F32),
            vmem((2, 8, 24, TILE), F32),
            vmem((2, 4, 2, 24, TILE), F32),
            vmem((2, up, COLS), BF16),
            vmem((2, up, COLS), BF16),
            vmem((2, up, COLS), BF16),
            vmem((2, 2, up, COLS), BF16),
            vmem((4, low, COLS), BF16),
            vmem((4, low, COLS), BF16),
            vmem((4, low, COLS), BF16),
            vmem((up, COLS), BF16),
            vmem((up, COLS), BF16),
            vmem((4, low, COLS), BF16),
            vmem((3, rows, COLS), F32),
            vmem((3,) + vision_states[0].shape, F32),
            vmem((2, 32, 5 * COLS), F32),
            vmem((8, 32, COLS), F32),
            vmem((3, ROWS, COLS), F32),
            vmem((2, 16, 5 * COLS), F32),
            vmem((2, 2, 16, TILE), BF16),
            vmem((8, 2, 16, TILE), BF16),
            vmem((2, ROWS, TILE), F32),
            vmem((rows, COLS), BF16),
            vmem((2,) + square, BF16),
            dma((5, 2)),
            dma((8,)),
            dma((3, 2)),
            dma((5, 2)), dma((5, 2)),
            dma((4, 6)), dma((4, 6)),
            dma((6, 4)), dma((6, 4)),
            dma((6, 4)), dma((6, 4)),
            dma((8,)), dma((8,)),
            dma((2, 8)), dma((2, 8)),
            dma((8,)), dma((8,)),
            dma((6,)), dma((6,)),
            dma((4,)), dma((4,)),
            dma((4,)), dma((4,)),
            dma((8,)), dma((8,)),
            dma((6, 4)), dma((6, 4)),
            dma((6, 4)), dma((6, 4)),
            dma((4, 6)), dma((4, 6)),
            dma((5, 4)), dma((5, 4)),
            dma((3, 6)), dma((3, 6)),
            dma,
        ],
        compiler_params=pltpu.CompilerParams(collective_id=1, has_side_effects=True, vmem_limit_bytes=40 << 20),
    )(*[pltpu.with_memory_space_constraint(array, pltpu.HBM) for array in (text, vision, *text_states, *vision_states)])


def finish_kernel(*refs):
    text, vision, text_full, vision_full = refs[:5], refs[5:10], refs[10], refs[11]
    outs, vision_w = refs[12:22], refs[21]
    text_made, vision_made, sem, tile_sem = refs[22:]
    text_w = outs[4]
    copies = [
        pltpu.make_async_copy(vision_full.at[layer, t], vision_w.at[layer, :, :, t * TILE : (t + 1) * TILE], tile_sem.at[layer, t])
        for layer in range(2)
        for t in range(10)
    ]
    copies.append(pltpu.make_async_copy(text_full, text_w, sem.at[1]))
    for copy in copies:
        copy.start()

    def one(i):
        rows = pl.ds(pl.multiple_of(i * 32, 32), 32)
        made = adam_step(*[ref[rows] for ref in text])
        for j in range(4):
            text_made[j, rows] = made[j]

    loop(0, text_made.shape[1] // 32, one)
    for j in range(4):
        copies.append(pltpu.make_async_copy(text_made.at[j], outs[j], sem.at[2 + j]))
        copies[-1].start()

    def row(r):
        made = adam_step(*[ref[r] for ref in vision])
        for j in range(4):
            vision_made[j, r] = made[j]

    loop(0, vision_made.shape[1], row)
    for j in range(4):
        copies.append(pltpu.make_async_copy(vision_made.at[j], outs[5 + j], sem.at[6 + j]))
        copies[-1].start()
    for copy in copies:
        copy.wait()


def finish(text, vision, text_full, vision_full):
    def like(array):
        return jax.ShapeDtypeStruct(array.shape, array.dtype)

    in_hbm, in_vmem = pl.BlockSpec(memory_space=pltpu.HBM), pl.BlockSpec(memory_space=pltpu.VMEM)
    return pl.pallas_call(
        finish_kernel,
        name="write_results",
        out_shape=(like(text[0]),) * 4
        + (like(text_full),)
        + (like(vision[0]),) * 4
        + (jax.ShapeDtypeStruct((2, GROUPS, ROWS, 5 * COLS), BF16),),
        in_specs=[in_vmem] * 10 + [in_hbm] * 2,
        out_specs=[in_hbm] * 10,
        scratch_shapes=[
            pltpu.VMEM((4,) + text[0].shape, F32),
            pltpu.VMEM((4,) + vision[0].shape, F32),
            pltpu.SemaphoreType.DMA((10,)),
            pltpu.SemaphoreType.DMA((2, 10)),
        ],
        compiler_params=pltpu.CompilerParams(vmem_limit_bytes=16 << 20),
    )(*text, *vision, text_full, vision_full)


def body(
    text_grads, text_master, text_moment, text_second, text_ref,
    vision_grads, vision_master, vision_moment, vision_second, vision_ref,
):
    layers, width = vision_grads.shape[1], vision_grads.shape[3]
    text_states = (text_moment, text_second, text_master, text_ref)
    vision_states = tuple(
        jnp.transpose(array, (1, 0, 2)) for array in (vision_moment, vision_second, vision_master, vision_ref)
    )
    text_total, vision_total, text_full, vision_full = step(
        text_grads[0], vision_grads.reshape(layers, GROUPS, ROWS, width), text_states[:3], vision_states[:3]
    )
    outs = finish((text_total,) + text_states, (vision_total,) + vision_states, text_full, vision_full)
    vision_out = tuple(jnp.transpose(array, (1, 0, 2)) for array in outs[5:9])
    return outs[:5] + vision_out + (outs[9].reshape(layers, width, width),)


def solution(mesh):
    owned = P("tensor", "dp")
    vision_owned = P(None, ("dp", "tensor"), None)
    return jax.shard_map(
        body,
        mesh=mesh,
        in_specs=(P("dp", "tensor", None),) + (owned,) * 4 + (P(("dp", "tensor"), None, None, None),) + (vision_owned,) * 4,
        out_specs=(owned,) * 4 + (P("tensor", None),) + (vision_owned,) * 4 + (P(),),
        check_vma=False,
    )
```

time: 80.6 us -> 77.6 us (0.963)
  Pallas kernels: 79.7 us -> 76.7 us
    pallas_call x1, Pallas kernels: 75.3 us -> 72.3 us  [step(): pl.pallas_call(kernel_of(step_kernel), name='sum_step_gather', out_shape=...]
where the time goes in v5:
time: 77.6 us; the launch traced here: 77.5 us
  Pallas kernels  76.7 us (99%)
  between operations  0.78 us (1%)
    pallas_call x1, Pallas kernels, step(): pl.pallas_call(kernel_of(step_kernel), name='sum_step_gather', out_shape=...  72.3 us
    pallas_call x1, Pallas kernels, finish(): pl.pallas_call(finish_kernel, name='write_results', out_shape=(like(text[...  4.36 us

profile of v5, /device:TPU:1, one launch (start us, length us, event | category | flops | bytes accessed | tf_op | source)
XLA Modules:
  0.0 77.5 jit_solution(1538837131931958401)
XLA Ops:
  0.6 0.0 copy-start.1
  0.7 0.0 copy-start
  0.7 0.0 copy-start.2
  0.7 0.0 copy-start.7
  0.7 0.0 copy-start.5
  0.7 0.0 copy-start.4
  0.7 0.0 copy-start.6
  0.7 0.0 copy-start.3
  0.7 72.3 %sum_step_gather.1 = (f32[512,256]{1,0:T(8,128)S(1)}, f32[10,2,1280]{2,1,0:T(2,128)S(1)}, bf16[512,2048]{1,0:T(8,128)(2,1)S(1)}, bf16[2,10,16,80,128]{4,3,2,1,0:T(8,128)(2,1)S(1)}) custom-call(bf16[512,2048]{1,0:T(8,128)(2,1)} %bitcast.19, bf16[2,16,80,1280]{3,2,1,0:T(8,128)(2,1)} %bitcast.18, f32[512,256]{1,0:T(8,128)} %refs_1_.3, f32[512,256]{1,0:T(8,128)} %refs_2_.3, ...), custom_call_target="tpu_custom_call" | custom-call | tf_op jit(solution)/shard_map/sum_step_gather/pallas_call | solution.py:840
  73.0 0.0 copy-done.1
  73.0 0.0 copy-done
  73.1 0.0 copy-done.2
  73.1 0.0 copy-done.7
  73.1 0.0 copy-done.5
  73.1 0.0 copy-done.4
  73.1 0.0 copy-done.6
  73.1 0.0 copy-done.3
  73.1 4.4 %write_results.1 = (f32[512,256]{1,0:T(8,128)}, f32[512,256]{1,0:T(8,128)}, f32[512,256]{1,0:T(8,128)}, f32[512,256]{1,0:T(8,128)}, bf16[512,2048]{1,0:T(8,128)(...) custom-call(f32[512,256]{1,0:T(8,128)S(1)} %get-tuple-element.24.ref, ...), custom_call_target="tpu_custom_call" | custom-call | tf_op jit(solution)/shard_map/write_results/pallas_call | solution.py:962
Async XLA Ops:
  0.6 72.4 %copy-start.1 = (f32[512,256]{1,0:T(8,128)S(1)}, f32[512,256]{1,0:T(8,128)}, u32[]{:S(2)}) copy-start(f32[512,256]{1,0:T(8,128)} %refs_2_.3) | copy-start | bytes 1572868
  0.7 72.4 %copy-start = (f32[512,256]{1,0:T(8,128)S(1)}, f32[512,256]{1,0:T(8,128)}, u32[]{:S(2)}) copy-start(f32[512,256]{1,0:T(8,128)} %refs_1_.3) | copy-start | bytes 1572868
  0.7 72.4 %copy-start.2 = (f32[512,256]{1,0:T(8,128)S(1)}, f32[512,256]{1,0:T(8,128)}, u32[]{:S(2)}) copy-start(f32[512,256]{1,0:T(8,128)} %refs_3_.1) | copy-start | bytes 1572868
  0.7 72.4 %copy-start.7 = (f32[2,10,1280]{2,0,1:T(2,128)S(1)}, f32[2,10,1280]{2,0,1:T(2,128)}, u32[]{:S(2)}) copy-start(f32[2,10,1280]{2,0,1:T(2,128)} %param.19) | copy-start | bytes 307204
  0.7 72.4 %copy-start.5 = (f32[2,10,1280]{2,0,1:T(2,128)S(1)}, f32[2,10,1280]{2,0,1:T(2,128)}, u32[]{:S(2)}) copy-start(f32[2,10,1280]{2,0,1:T(2,128)} %param.18) | copy-start | bytes 307204
  0.7 72.4 %copy-start.4 = (f32[2,10,1280]{2,0,1:T(2,128)S(1)}, f32[2,10,1280]{2,0,1:T(2,128)}, u32[]{:S(2)}) copy-start(f32[2,10,1280]{2,0,1:T(2,128)} %param.17) | copy-start | bytes 307204
  0.7 72.4 %copy-start.6 = (f32[2,10,1280]{2,0,1:T(2,128)S(1)}, f32[2,10,1280]{2,0,1:T(2,128)}, u32[]{:S(2)}) copy-start(f32[2,10,1280]{2,0,1:T(2,128)} %param.16) | copy-start | bytes 307204
  0.7 72.4 %copy-start.3 = (f32[512,256]{1,0:T(8,128)S(1)}, f32[512,256]{1,0:T(8,128)}, u32[]{:S(2)}) copy-start(f32[512,256]{1,0:T(8,128)} %refs_4_.1) | copy-start | bytes 1572868

commit v6 on v5

--- a/solution.py
+++ b/solution.py
@@ -448,12 +448,13 @@
     def state_copy(i):
         to, py, pc = near.line[i]
         return remote(
-            own_state.at[pc, :, columns(py, COLS)], line_state.at[y * 2 + core], state_s.at[i], state_r.at[i], to
+            own_state.at[pc, pl.ds(0, 32), columns(py, COLS)], line_state.at[y * 2 + core, pl.ds(0, 32)], state_s.at[i],
+            state_r.at[i], to,
         )
 
     def send_states():
         each(1, 8, lambda i: state_copy(i).start())
-        line_state[y * 2 + core] = own_state[core, :, columns(y, COLS)]
+        line_state[y * 2 + core, :32] = own_state[core, :32, columns(y, COLS)]
 
     def join_states():
         each(1, 8, lambda i: state_copy(i).wait_recv())
@@ -547,7 +548,7 @@
         for tile in range(2):
             for i in range(8):
                 packed[tile, 10 * i : 10 * i + 10, :] = line_rest[i, tile].astype(F32)[:10]
-            plane_rest[near.a, near.b, tile * ROWS : (tile + 1) * ROWS] = packed[tile].astype(BF16)
+            plane_rest[near.a, near.b, tile * ROWS : (tile + 1) * ROWS] = packed[tile, :ROWS].astype(BF16)
         each(1, 4, lambda k: plane1(0, k).start())
 
     def across(unit):
@@ -842,7 +843,7 @@
         name="sum_step_gather",
         out_shape=(
             jax.ShapeDtypeStruct((rows, COLS), F32),
-            jax.ShapeDtypeStruct(vision_states[0].shape, F32),
+            jax.ShapeDtypeStruct((16,) + vision_states[0].shape[1:], F32),
             jax.ShapeDtypeStruct((rows, 8 * COLS), BF16),
             jax.ShapeDtypeStruct((2, 10) + tile, BF16),
         ),
@@ -881,14 +882,14 @@
             vmem((up, COLS), BF16),
             vmem((4, low, COLS), BF16),
             vmem((3, rows, COLS), F32),
-            vmem((3,) + vision_states[0].shape, F32),
-            vmem((2, 32, 5 * COLS), F32),
-            vmem((8, 32, COLS), F32),
-            vmem((3, ROWS, COLS), F32),
-            vmem((2, 16, 5 * COLS), F32),
+            vmem((4,) + vision_states[0].shape, F32),
+            vmem((2, 40, 5 * COLS), F32),
+            vmem((8, 40, COLS), F32),
+            vmem((3, ROWS + 8, COLS), F32),
+            vmem((2, 24, 5 * COLS), F32),
             vmem((2, 2, 16, TILE), BF16),
             vmem((8, 2, 16, TILE), BF16),
-            vmem((2, ROWS, TILE), F32),
+            vmem((2, ROWS + 8, TILE), F32),
             vmem((rows, COLS), BF16),
             vmem((2,) + square, BF16),
             dma((5, 2)),
@@ -919,7 +920,7 @@
 def finish_kernel(*refs):
     text, vision, text_full, vision_full = refs[:5], refs[5:10], refs[10], refs[11]
     outs, vision_w = refs[12:22], refs[21]
-    text_made, vision_made, sem, tile_sem = refs[22:]
+    text_made, vision_made, vision_in, sem, tile_sem, in_sem = refs[22:]
     text_w = outs[4]
     copies = [
         pltpu.make_async_copy(vision_full.at[layer, t], vision_w.at[layer, :, :, t * TILE : (t + 1) * TILE], tile_sem.at[layer, t])
@@ -927,7 +928,9 @@
         for t in range(10)
     ]
     copies.append(pltpu.make_async_copy(text_full, text_w, sem.at[1]))
-    for copy in copies:
+    rows_in = vision_made.shape[1]
+    taken = [pltpu.make_async_copy(ref.at[:rows_in], vision_in.at[k], in_sem.at[k]) for k, ref in enumerate(vision)]
+    for copy in taken + copies:
         copy.start()
 
     def one(i):
@@ -941,8 +944,11 @@
         copies.append(pltpu.make_async_copy(text_made.at[j], outs[j], sem.at[2 + j]))
         copies[-1].start()
 
+    for copy in taken:
+        copy.wait()
+
     def row(r):
-        made = adam_step(*[ref[r] for ref in vision])
+        made = adam_step(*[vision_in[k, r] for k in range(5)])
         for j in range(4):
             vision_made[j, r] = made[j]
 
@@ -964,15 +970,17 @@
         name="write_results",
         out_shape=(like(text[0]),) * 4
         + (like(text_full),)
-        + (like(vision[0]),) * 4
+        + (like(vision[1]),) * 4
         + (jax.ShapeDtypeStruct((2, GROUPS, ROWS, 5 * COLS), BF16),),
-        in_specs=[in_vmem] * 10 + [in_hbm] * 2,
+        in_specs=[in_vmem] * 5 + [in_hbm] * 7,
         out_specs=[in_hbm] * 10,
         scratch_shapes=[
             pltpu.VMEM((4,) + text[0].shape, F32),
-            pltpu.VMEM((4,) + vision[0].shape, F32),
+            pltpu.VMEM((5,) + vision[1].shape, F32),
+            pltpu.VMEM((6,) + vision[1].shape, F32),
             pltpu.SemaphoreType.DMA((10,)),
             pltpu.SemaphoreType.DMA((2, 10)),
+            pltpu.SemaphoreType.DMA((5,)),
         ],
         compiler_params=pltpu.CompilerParams(vmem_limit_bytes=16 << 20),
     )(*text, *vision, text_full, vision_full)

time: 77.6 us -> 78.3 us (level)
  no operation moved by 1% of the time
where the time goes in v6:
time: 78.3 us; the launch traced here: 78.2 us
  Pallas kernels  77.4 us (99%)
    pallas_call x1, Pallas kernels, step(): pl.pallas_call(kernel_of(step_kernel), name='sum_step_gather', out_shape=...  72.3 us
    pallas_call x1, Pallas kernels, finish(): pl.pallas_call(finish_kernel, name='write_results', out_shape=(like(text[...  5.09 us

profile of v6, /device:TPU:1, one launch (start us, length us, event | category | flops | bytes accessed | tf_op | source)
XLA Modules:
  0.0 78.2 jit_solution(9205179555650619749)
XLA Ops:
  0.6 0.0 copy-start.1
  0.7 0.0 copy-start
  0.7 0.0 copy-start.2
  0.7 0.0 copy-start.7
  0.7 0.0 copy-start.5
  0.7 0.0 copy-start.4
  0.7 0.0 copy-start.6
  0.7 0.0 copy-start.3
  0.7 72.3 %sum_step_gather.1 = (f32[512,256]{1,0:T(8,128)S(1)}, f32[16,2,1280]{2,1,0:T(2,128)S(1)}, bf16[512,2048]{1,0:T(8,128)(2,1)S(1)}, bf16[2,10,16,80,128]{4,3,2,1,0:T(8,128)(2,1)S(1)}) custom-call(bf16[512,2048]{1,0:T(8,128)(2,1)} %bitcast.19, bf16[2,16,80,1280]{3,2,1,0:T(8,128)(2,1)} %bitcast.18, f32[512,256]{1,0:T(8,128)} %refs_1_.3, f32[512,256]{1,0:T(8,128)} %refs_2_.3, ...), custom_call_target="tpu_custom_call" | custom-call | tf_op jit(solution)/shard_map/sum_step_gather/pallas_call | solution.py:841
  73.0 0.0 copy-done.1
  73.0 0.0 copy-done
  73.1 0.0 copy-done.2
  73.1 0.0 copy-done.7
  73.1 0.0 copy-done.5
  73.1 0.0 copy-done.4
  73.1 0.0 copy-done.6
  73.1 0.0 copy-done.3
  73.1 5.1 %write_results.1 = (f32[512,256]{1,0:T(8,128)}, f32[512,256]{1,0:T(8,128)}, f32[512,256]{1,0:T(8,128)}, f32[512,256]{1,0:T(8,128)}, bf16[512,2048]{1,0:T(8,128)(...) custom-call(f32[512,256]{1,0:T(8,128)S(1)} %get-tuple-element.24.ref, ...), custom_call_target="tpu_custom_call" | custom-call | tf_op jit(solution)/shard_map/write_results/pallas_call | solution.py:968
Async XLA Ops:
  0.6 72.4 %copy-start.1 = (f32[512,256]{1,0:T(8,128)S(1)}, f32[512,256]{1,0:T(8,128)}, u32[]{:S(2)}) copy-start(f32[512,256]{1,0:T(8,128)} %refs_2_.3) | copy-start | bytes 1572868
  0.7 72.4 %copy-start = (f32[512,256]{1,0:T(8,128)S(1)}, f32[512,256]{1,0:T(8,128)}, u32[]{:S(2)}) copy-start(f32[512,256]{1,0:T(8,128)} %refs_1_.3) | copy-start | bytes 1572868
  0.7 72.4 %copy-start.2 = (f32[512,256]{1,0:T(8,128)S(1)}, f32[512,256]{1,0:T(8,128)}, u32[]{:S(2)}) copy-start(f32[512,256]{1,0:T(8,128)} %refs_3_.1) | copy-start | bytes 1572868
  0.7 72.4 %copy-start.7 = (f32[2,10,1280]{2,0,1:T(2,128)S(1)}, f32[2,10,1280]{2,0,1:T(2,128)}, u32[]{:S(2)}) copy-start(f32[2,10,1280]{2,0,1:T(2,128)} %param.19) | copy-start | bytes 307204
  0.7 72.4 %copy-start.5 = (f32[2,10,1280]{2,0,1:T(2,128)S(1)}, f32[2,10,1280]{2,0,1:T(2,128)}, u32[]{:S(2)}) copy-start(f32[2,10,1280]{2,0,1:T(2,128)} %param.18) | copy-start | bytes 307204
  0.7 72.4 %copy-start.4 = (f32[2,10,1280]{2,0,1:T(2,128)S(1)}, f32[2,10,1280]{2,0,1:T(2,128)}, u32[]{:S(2)}) copy-start(f32[2,10,1280]{2,0,1:T(2,128)} %param.17) | copy-start | bytes 307204
  0.7 72.4 %copy-start.6 = (f32[2,10,1280]{2,0,1:T(2,128)S(1)}, f32[2,10,1280]{2,0,1:T(2,128)}, u32[]{:S(2)}) copy-start(f32[2,10,1280]{2,0,1:T(2,128)} %param.16) | copy-start | bytes 307204
  0.7 72.4 %copy-start.3 = (f32[512,256]{1,0:T(8,128)S(1)}, f32[512,256]{1,0:T(8,128)}, u32[]{:S(2)}) copy-start(f32[512,256]{1,0:T(8,128)} %refs_4_.1) | copy-start | bytes 1572868
